TPU v7x, 32 devices: a whole 2x2x4 slice. The times are simulated.
32 devices in a mesh: elem: 8 (over z, x), blk: 4 (over y, core).
Axes of the slice: x: 2, y: 2, z: 4, core: 2. Of those that a mesh axis runs over, the one named last changes fastest.
Arguments:
- basis: bfloat16 [4096, 3, 512], P('elem'), may hold values from -6 to 6
- send_rows: int32 [8, 4, 256], P('elem', 'blk'), may hold values from 0 to 511
- elem_slot: int32 [8, 2048], P(None, ('elem', 'blk')), may hold values from 0 to 255, as said below
- set_size: int32 [8], replicated, may hold values from 1 to 256, 1280 in all
- elem_weight: float32 [2048], P(('elem', 'blk')), may hold values from 0.2 to 5
- element_stiffening: float32 [2048], P(('elem', 'blk')), may hold values from 1 to 8
- state: bfloat16 [512], replicated, may hold values from -0.25 to 0.25
- load: float32 [512], P('blk'), may hold values from -6 to 6
Outputs:
- tangent: float32 [512, 512], P('elem', 'blk')
- residual: float32 [512], P('blk')
Inputs may be any that keep to these rules, and one draw needn't show every extreme that they name: `elem_slot`: for element column of device (s, b): p names slot p % 32 of what owner p // 32 sends to that device. From each owner only its first n slots are named, n at most 32; for every device exactly one owner gives 32, and the n over all owners sum to 128.
All inputs are finite; a program needn't handle non-finite values.
Results may differ from a plain program's by a relative error of at most 0.0003.
Values may be sent and summed in bfloat16 or wider, within the bound.
A program may use at most 64 MiB of HBM per device.

v0:
```python
import jax
import jax.numpy as jnp
from jax import lax
from jax.sharding import PartitionSpec as P


def corner_grads():
    corner = jnp.arange(8)[:, None]
    bit = corner // 2 ** jnp.arange(3)[None, :] % 2
    return (bit * 2 - 1).astype(jnp.float32) * 0.25


def element_contributions(basis_matrix, displacement, stiffening_power):
    grads = corner_grads()
    element_count = basis_matrix.shape[0]
    basis_modes = basis_matrix.shape[2]
    corner_nodes = basis_matrix.reshape(element_count, 8, 3, basis_modes)
    grad_basis = jnp.einsum(
        "ak,eacm->ekcm",
        grads.astype(jnp.bfloat16),
        corner_nodes,
        preferred_element_type=jnp.float32,
    )
    moved = displacement.reshape(8, 3, element_count)
    hgrad = jnp.einsum("ak,ace->kce", grads, moved, precision=lax.Precision.HIGHEST)
    volume = hgrad[0, 0] + hgrad[1, 1] + hgrad[2, 2]
    stiff = 1.0 + stiffening_power * volume**2 - 2.0 / 3.0
    press = volume + stiffening_power * volume**3 / 3.0 - 2.0 / 3.0 * volume
    eye = jnp.eye(3, dtype=jnp.float32)
    stress = hgrad + jnp.transpose(hgrad, (1, 0, 2)) + press[None, None, :] * eye[:, :, None]
    force_vector = (
        jnp.einsum("ak,kce->ace", grads, stress, precision=lax.Precision.HIGHEST).reshape(
            24, element_count
        )
        + 0.25 * displacement
    )
    sym = grad_basis + jnp.transpose(grad_basis, (0, 2, 1, 3))
    trace_basis = grad_basis[:, 0, 0] + grad_basis[:, 1, 1] + grad_basis[:, 2, 2]
    mode_image = jnp.einsum("ak,ekcm->eacm", grads, sym, precision=lax.Precision.HIGHEST)
    mode_image = (
        mode_image
        + stiff[:, None, None, None] * grads[None, :, :, None] * trace_basis[:, None, None, :]
        + 0.25 * corner_nodes.astype(jnp.float32)
    )
    return (mode_image.reshape(element_count, 24, basis_modes), force_vector)


def local(basis, send_rows, elem_slot, set_size, elem_weight, element_stiffening, state, load):
    nodes = basis.shape[0]
    basis_modes = basis.shape[2]
    flat = basis.reshape(nodes, 3 * basis_modes)
    outgoing = jnp.take(flat, send_rows[0, 0], axis=0)
    arrived = lax.all_to_all(outgoing, "elem", split_axis=0, concat_axis=0, tiled=True)
    element_count = elem_slot.shape[1]
    chosen_elements = jnp.take(arrived, elem_slot.T.reshape(-1), axis=0)
    basis_matrix = chosen_elements.reshape(element_count, 24, basis_modes)
    set_index = lax.axis_index("elem")
    block_index = lax.axis_index("blk")
    live = lax.dynamic_index_in_dim(set_size, set_index, keepdims=False)
    position = block_index * element_count + jnp.arange(element_count, dtype=jnp.int32)
    weights = jnp.where(position < live, elem_weight, jnp.zeros_like(elem_weight))
    displacement = jnp.einsum("agd,d->ga", basis_matrix, state, preferred_element_type=jnp.float32)
    mode_image, force_vector = element_contributions(basis_matrix, displacement, element_stiffening)
    weighted_image = (weights[:, None, None] * mode_image).astype(jnp.bfloat16)
    weighted_force = (force_vector * weights[None, :]).astype(jnp.bfloat16)
    tangent = lax.dot_general(
        basis_matrix,
        weighted_image,
        (((0, 1), (0, 1)), ((), ())),
        preferred_element_type=jnp.float32,
    )
    force_all = lax.dot_general(
        basis_matrix,
        weighted_force,
        (((0, 1), (1, 0)), ((), ())),
        preferred_element_type=jnp.float32,
    )
    halfway, force_part = (
        lax.psum_scatter(tangent, "blk", scatter_dimension=1, tiled=True),
        lax.psum_scatter(force_all, "blk", scatter_dimension=0, tiled=True),
    )
    mine = lax.psum_scatter(halfway, "elem", scatter_dimension=0, tiled=True)
    force_cols = lax.psum(force_part, "elem")
    scale = lax.rsqrt(24.0 * jnp.sum(set_size).astype(jnp.float32))
    return (mine * scale, force_cols * scale - load)


def solution(mesh):
    in_specs = (
        P("elem", None, None),
        P("elem", "blk", None),
        P(None, ("elem", "blk")),
        P(),
        P(("elem", "blk")),
        P(("elem", "blk")),
        P(),
        P("blk"),
    )
    out_specs = (P("elem", "blk"), P("blk"))
    return jax.shard_map(local, mesh=mesh, in_specs=in_specs, out_specs=out_specs, check_vma=False)
```

profile of v0, /device:TPU:0, one launch (start us, length us, event | category | flops | bytes accessed | tf_op | source)
XLA Modules:
  0.0 163.8 jit_solution(5221475504157914889)
XLA Ops:
  7.2 1.7 %copy.30 = bf16[512,3,512]{0,2,1:T(8,128)(2,1)S(1)} copy(bf16[512,3,512]{2,0,1:T(8,128)(2,1)} %param.8) | data formatting | bytes 3145728 | tf_op args[0]
  8.9 0.7 copy.31
  10.9 1.3 gather_fusion
  12.2 1.0 broadcast_select_fusion.6
  13.2 7.3 %all-to-all-start = ((bf16[8,32,1536]{2,1,0:T(8,128)(2,1)}), bf16[8,32,1536]{2,1,0:T(8,128)(2,1)S(1)}, u32[]{:S(2)}, u32[]{:S(2)}) async-start(bf16[8,32,1536]{2,1,0:T(8,128)(2,1)} %broadcast_select_fusion.6), calls=%async_computation | async-start | bytes 1572864 | tf_op jit(solution)/shard_map/all_to_all | solution.py:53
  21.3 0.9 broadcast_in_dim.51
  23.7 17.0 %all-to-all-done = bf16[8,32,1536]{2,1,0:T(8,128)(2,1)S(1)} async-done(((bf16[8,32,1536]{2,1,0:T(8,128)(2,1)}), bf16[8,32,1536]{2,1,0:T(8,128)(2,1)S(1)}, u32[]{:S(2)}, u32[]{:S(2)}) %all-to-all-start) | async-done | bytes 786464 | tf_op jit(solution)/shard_map/all_to_all | solution.py:53
  40.7 2.1 %gather_fusion.1 = bf16[512,1536]{1,0:T(8,128)(2,1)S(1)} fusion(bf16[256,1536]{1,0:T(8,128)(2,1)S(1)} %bitcast.68, s32[1024]{0:T(1024)S(1)} %pad_clamp_fusion), kind=kCustom, calls=%fused_computation.1 | custom fusion | bytes 3147776 | tf_op jit(solution)/shard_map/jit(_take)/gather | solution.py:55
  42.8 1.6 %gather.18 = bf16[64,24,512]{2,1,0:T(8,128)(2,1)} reshape(bf16[512,1536]{1,0:T(8,128)(2,1)S(1)} %gather_fusion.1) | data formatting | bytes 3145728 | tf_op jit(solution)/shard_map/jit(_take)/gather | solution.py:55
  44.5 0.8 fusion.8
  45.2 1.8 %copy.62 = f32[64,3,512,3]{2,1,3,0:T(4,128)} copy(f32[64,3,512,3]{2,3,1,0:T(4,128)S(1)} %fusion.8) | data formatting | bytes 2359296 | tf_op jit(solution)/shard_map/ak,eacm->ekcm/dot_general | solution.py:18
  47.0 2.0 %bitcast_add_fusion.1 = f32[64,3,3,512]{3,2,1,0:T(4,128)} fusion(f32[64,3,512,3]{2,3,1,0:T(4,128)S(1)} %fusion.8), kind=kLoop, calls=%fused_computation.6 | loop fusion | flops 294912 | bytes 2359296 | tf_op jit(solution)/shard_map/add | solution.py:37
  49.0 1.5 fusion.7
  51.0 1.7 %slice_add_fusion = f32[64,1,1,512]{3,2,1,0:T(1,128)S(1)} fusion(f32[64,3,3,512]{3,2,1,0:T(4,128)} %bitcast.73), kind=kLoop, calls=%fused_computation.22 | loop fusion | flops 65536 | bytes 524288 | tf_op jit(solution)/shard_map/add | solution.py:38
  52.8 5.8 %fusion.2 = bf16[64,8,3,512]{3,1,2,0:T(8,128)(2,1)S(1)} fusion(f32[64,3,3,512]{3,2,1,0:T(4,128)} %bitcast_add_fusion.1, f32[64,512]{1,0:T(8,128)S(1)} %bitcast.75, f32[64,8,3]{1,2,0:T(4,128)S(1)} %broadcast_multiply_fusion, f32[64]{0:T(128)S(1)} %compare_select_fusion.10, bf16[64,8,3,512]{3,1,2,0:T(8,128)(2,1)S(1)} %bitcast.70, pred[64,8]{1,0:T(8,128)(4,1)S(1)} %copy.33, ...), kind=kOutput, calls=%fused_computation.5 | convolution fusion | flops 34603536 | bytes 4463416 | tf_op jit(solution)/shard_map/ak,ekcm->eacm/dot_general | solution.py:39
  58.6 1.7 %copy.37 = bf16[64,8,3,512]{3,0,2,1:T(8,128)(2,1)} copy(bf16[64,8,3,512]{3,1,2,0:T(8,128)(2,1)S(1)} %fusion.2) | data formatting | bytes 3145728 | tf_op jit(solution)/shard_map/convert_element_type | solution.py:64
  60.3 1.3 broadcast_select_fusion.5
  61.6 2.7 %select_n.226 = bf16[64,24,512]{2,1,0:T(8,128)(2,1)S(1)} reshape(bf16[512,1536]{1,0:T(8,128)(2,1)} %broadcast_select_fusion.5) | data formatting | bytes 3145728 | tf_op jit(solution)/shard_map/jit(_take)/select_n | solution.py:55
  64.3 2.2 %fusion.9 = f32[512,512]{1,0:T(8,128)} fusion(bf16[64,24,512]{2,1,0:T(8,128)(2,1)S(1)} %select_n.226, bf16[64,24,512]{2,0,1:T(8,128)(2,1)S(1)} %bitcast.74), kind=kOutput, calls=%fused_computation.16 | convolution fusion | flops 805306368 | bytes 4194304 | tf_op jit(solution)/shard_map/dot_general | solution.py:66
  69.7 20.9 %reduce-scatter.3.cloned.1.call-done = f32[512,128]{1,0:T(8,128)} async-done(((f32[512,512]{1,0:T(8,128)}), f32[512,128]{1,0:T(8,128)}) %reduce-scatter.3.cloned.1.call-update) | async-done | bytes 262160 | tf_op jit(solution)/shard_map/reduce_scatter | solution.py:79
  91.2 5.7 %all-reduce = f32[512]{0:T(512)S(1)} all-reduce(f32[512]{0:T(512)S(1)} %bitcast.80), channel_id=4, replica_groups=mesh['elem'=8,'blk'=4] {'blk'}, use_global_device_ids=true, to_apply=%region_3.4.clone | all-reduce | flops 512 | bytes 4096
  97.0 21.5 %psum.7 = f32[128]{0:T(128)S(1)} all-reduce(f32[128]{0:T(128)S(1)} %dynamic-slice.1), channel_id=1, replica_groups=mesh['elem'=8,'blk'=4] {'elem'}, use_global_device_ids=true, to_apply=%region_4.5 | all-reduce | flops 128 | bytes 1024 | tf_op jit(solution)/shard_map/psum | solution.py:83
  119.1 36.5 %reduce-scatter.5.cloned.1.call-done = f32[64,128]{1,0:T(8,128)} async-done(((f32[512,128]{1,0:T(8,128)}), f32[64,128]{1,0:T(8,128)}) %reduce-scatter.5.cloned.1.call-update) | async-done | bytes 32784 | tf_op jit(solution)/shard_map/reduce_scatter | solution.py:82
  155.6 1.4 broadcast_multiply_fusion.1
  (66 shorter events, 7.0 us)
Async XLA Ops:
  8.9 0.7 copy-start.4
  12.2 8.4 %copy-start.3 = (s32[8,64]{1,0:T(8,128)S(1)}, s32[8,64]{1,0:T(8,128)}, u32[]{:S(2)}) copy-start(s32[8,64]{1,0:T(8,128)} %param.10) | copy-start | bytes 6148
  12.2 8.8 %copy-start.5 = (bf16[512]{0:T(512)(128)(2,1)S(1)}, bf16[512]{0:T(512)(128)(2,1)}, u32[]{:S(2)}) copy-start(bf16[512]{0:T(512)(128)(2,1)} %param.14) | copy-start | bytes 3076
  13.2 27.4 %all-to-all-start = ((bf16[8,32,1536]{2,1,0:T(8,128)(2,1)}), bf16[8,32,1536]{2,1,0:T(8,128)(2,1)S(1)}, u32[]{:S(2)}, u32[]{:S(2)}) async-start(bf16[8,32,1536]{2,1,0:T(8,128)(2,1)} %broadcast_select_fusion.6), calls=%async_computation | async-start | bytes 1572864 | tf_op jit(solution)/shard_map/all_to_all | solution.py:53
  20.5 1.7 %copy-start.9 = (s32[8]{0:T(128)S(1)}, s32[8]{0:T(128)}, u32[]{:S(2)}) copy-start(s32[8]{0:T(128)} %param.11) | copy-start | bytes 100
  20.5 2.3 %copy-start.6 = (f32[64]{0:T(128)S(1)}, f32[64]{0:T(128)}, u32[]{:S(2)}) copy-start(f32[64]{0:T(128)} %param.12) | copy-start | bytes 772
  20.5 70.1 %reduce-scatter.3.cloned.1.call-start = ((), (), s32[]{:S(2)}) async-start(), calls=%async_computation.3 | async-start | bytes 1310720 | tf_op jit(solution)/shard_map/reduce_scatter | solution.py:79
  47.0 2.0 %copy-start = (bf16[64,24,512]{2,1,0:T(8,128)(2,1)S(1)}, bf16[64,24,512]{2,1,0:T(8,128)(2,1)}, u32[]{:S(2)}) copy-start(bf16[64,24,512]{2,1,0:T(8,128)(2,1)} %gather.18) | copy-start | bytes 4718596
  49.0 1.9 %copy-start.7 = (f32[64]{0:T(128)S(1)}, f32[64]{0:T(128)}, u32[]{:S(2)}) copy-start(f32[64]{0:T(128)} %param.13) | copy-start | bytes 772
  61.6 2.7 %copy-start.2 = (bf16[64,8,3,512]{3,0,2,1:T(8,128)(2,1)S(1)}, bf16[64,8,3,512]{3,0,2,1:T(8,128)(2,1)}, u32[]{:S(2)}) copy-start(bf16[64,8,3,512]{3,0,2,1:T(8,128)(2,1)} %copy.37) | copy-start | bytes 4718596
  64.3 3.6 %copy-start.10 = (u32[32]{0:T(128)S(1)}, u32[32]{0:T(128)}, u32[]{:S(2)}) copy-start(u32[32]{0:T(128)} %constant.111) | copy-start | bytes 388
  66.6 24.2 %copy-start.1 = (bf16[64,24,512]{2,1,0:T(8,128)(2,1)S(1)}, bf16[64,24,512]{2,1,0:T(8,128)(2,1)}, u32[]{:S(2)}) copy-start(bf16[64,24,512]{2,1,0:T(8,128)(2,1)} %gather.18) | copy-start | bytes 4718596
  66.6 89.0 %reduce-scatter.5.cloned.1.call-start = ((), (), s32[]{:S(2)}) async-start(), calls=%async_computation.4 | async-start | bytes 294912 | tf_op jit(solution)/shard_map/reduce_scatter | solution.py:82
  90.6 27.9 %copy-start.8 = (f32[128]{0:T(128)S(1)}, f32[128]{0:T(128)}, u32[]{:S(2)}) copy-start(f32[128]{0:T(128)} %param.15) | copy-start | bytes 1540
Sparse Core Ops, SparseCore 0:
  66.7 23.8 reduce-scatter.2
  94.3 61.2 reduce-scatter.4
where the time goes:
time: 164 us
  waiting for transfers between devices  74.5 us (45%)
  blocking collectives  27.2 us (17%)
  local copies, waits for them, and re-layouts  17.3 us (11%)
  between operations  15.7 us (10%)
  matrix products  11.5 us (7%)
  other arithmetic  10.2 us (6%)
  starting transfers between devices  7.34 us (4%)
    reduce_scatter x1, waiting for transfers between devices, local(): mine = lax.psum_scatter(halfway, 'elem', scatter_dimension=0, tiled=True)  36.5 us
    psum x1, blocking collectives, local(): force_cols = lax.psum(force_part, 'elem')  21.5 us
    reduce_scatter x1, waiting for transfers between devices, local(): lax.psum_scatter(tangent, 'blk', scatter_dimension=1, tiled=True)  20.9 us
    all_to_all x1, waiting for transfers between devices, local(): lax.all_to_all(outgoing, 'elem', split_axis=0, concat_axis=0, tiled=True)  17 us
    all_to_all x1, starting transfers between devices, local(): lax.all_to_all(outgoing, 'elem', split_axis=0, concat_axis=0, tiled=True)  7.26 us
    dot_general x1, matrix products, element_contributions(): jnp.einsum('ak,ekcm->eacm', grads, sym, precision=lax.Precision.HIGHEST)  5.82 us
    unnamed x1, blocking collectives  5.73 us
    gather x2, local copies, waits for them, and re-layouts, local(): chosen_elements = jnp.take(arrived, elem_slot.T.reshape(-1), axis=0)  3.77 us
  transfers between devices with their start and end apart: 3, of which 3 were waited for; matrix products, arithmetic and copies ran while one was open for 4% of the time, Pallas kernels for 0%

commit v1 on v0

--- a/solution.py
+++ b/solution.py
@@ -1,7 +1,14 @@
+import functools
+
 import jax
 import jax.numpy as jnp
 from jax import lax
+from jax.experimental import pallas as pl
+from jax.experimental.pallas import tpu as pltpu
 from jax.sharding import PartitionSpec as P
+
+LANES = 128
+MESH = pl.DeviceIdType.MESH
 
 
 def corner_grads():
@@ -85,6 +92,336 @@
     return (mine * scale, force_cols * scale - load)
 
 
+def signs(corner):
+    return [1.0 if corner >> axis & 1 else -1.0 for axis in range(3)]
+
+
+def signed_sum(terms, sign):
+    total = terms[0] if sign[0] > 0 else -terms[0]
+    for term, one in zip(terms[1:], sign[1:]):
+        total = total + term if one > 0 else total - term
+    return total
+
+
+def fused_kernel(
+    devs,
+    basis_ref,
+    send_ref,
+    slot_ref,
+    size_ref,
+    aux_ref,
+    state_ref,
+    load_ref,
+    tangent_ref,
+    residual_ref,
+    out_rows,
+    arr,
+    v_ref,
+    vt_ref,
+    w_ref,
+    g_ref,
+    part,
+    recv_core,
+    mid,
+    recv_first,
+    recv_second,
+    acc,
+    recv_z,
+    gather_send,
+    gather_recv,
+    core_send,
+    core_recv,
+    first_send,
+    first_recv,
+    second_send,
+    second_recv,
+    z_send,
+    z_recv,
+):
+    nodes = basis_ref.shape[1]
+    modes = basis_ref.shape[2]
+    slots = arr.shape[1]
+    cap = slots // devs
+    elements = aux_ref.shape[1] // 2
+    corners = 8 * elements
+    planes = devs // 2
+    rows = modes // devs
+    me = lax.axis_index("elem")
+    blk = lax.axis_index("blk")
+    x, z = lax.rem(me, 2), me // 2
+    core, y = lax.rem(blk, 2), blk // 2
+    core_peer = (me, y * 2 + 1 - core)
+    y_peer = (me, (1 - y) * 2 + core)
+    x_peer = (z * 2 + 1 - x, blk)
+
+    barrier = pltpu.get_barrier_semaphore()
+    for step in range(1, devs):
+        pl.semaphore_signal(
+            barrier, inc=1, device_id=(lax.rem(me + step, devs), blk), device_id_type=MESH
+        )
+    for peer in (core_peer, y_peer):
+        pl.semaphore_signal(barrier, inc=1, device_id=peer, device_id_type=MESH)
+
+    asked = jnp.broadcast_to(send_ref[...], (nodes, slots))
+    pick_t = jnp.where(lax.broadcasted_iota(jnp.int32, (nodes, slots), 0) == asked, 1.0, 0.0)
+    pick = jnp.transpose(pick_t).astype(jnp.bfloat16)
+    for c in range(3):
+        out_rows[c] = jnp.dot(
+            pick, basis_ref[c], preferred_element_type=jnp.float32
+        ).astype(jnp.bfloat16)
+
+    pl.semaphore_wait(barrier, devs + 1)
+    mine = pl.ds(pl.multiple_of(me * cap, cap), cap)
+    copies = []
+    for step in range(1, devs):
+        dest = lax.rem(me + step, devs)
+        copy = pltpu.make_async_remote_copy(
+            src_ref=out_rows.at[:, pl.ds(pl.multiple_of(dest * cap, cap), cap), :],
+            dst_ref=arr.at[:, mine, :],
+            send_sem=gather_send.at[step - 1],
+            recv_sem=gather_recv.at[step - 1],
+            device_id=(dest, blk),
+            device_id_type=MESH,
+        )
+        copy.start()
+        copies.append(copy)
+    arr[:, mine, :] = out_rows[:, mine, :]
+
+    wanted = jnp.broadcast_to(slot_ref[...], (slots, corners))
+    spread_t = jnp.where(lax.broadcasted_iota(jnp.int32, (slots, corners), 0) == wanted, 1.0, 0.0)
+    spread = jnp.transpose(spread_t)
+    spread_t = spread_t.astype(jnp.bfloat16)
+    by_corner = [spread[a * elements : (a + 1) * elements] for a in range(8)]
+    coef = jnp.concatenate(
+        [0.25 * signed_sum(by_corner, [signs(a)[k] for a in range(8)]) for k in range(3)], axis=0
+    ).astype(jnp.bfloat16)
+    spread = spread.astype(jnp.bfloat16)
+    columns = jnp.transpose(jnp.broadcast_to(aux_ref[...], (LANES, 2 * elements)))
+    live = size_ref[me]
+    position = blk * elements + lax.broadcasted_iota(jnp.int32, (elements, LANES), 0)
+    omega = jnp.where(position < live, columns[:elements], 0.0)
+    stiffening = columns[elements:]
+    state_rows = jnp.broadcast_to(state_ref[...].astype(jnp.float32), (LANES, modes)).astype(
+        jnp.bfloat16
+    )
+    for copy in copies:
+        copy.wait()
+
+    disp = []
+    for c in range(3):
+        rows_c = arr[c]
+        v = jnp.dot(spread, rows_c, preferred_element_type=jnp.float32).astype(jnp.bfloat16)
+        v_ref[c] = v
+        vt_ref[c] = lax.dot_general(
+            rows_c, spread_t, (((0,), (0,)), ((), ())), preferred_element_type=jnp.float32
+        ).astype(jnp.bfloat16)
+        g_ref[c] = jnp.dot(coef, rows_c, preferred_element_type=jnp.float32)
+        moved = lax.dot_general(
+            v, state_rows, (((1,), (1,)), ((), ())), preferred_element_type=jnp.float32
+        )
+        disp.append([moved[a * elements : (a + 1) * elements] for a in range(8)])
+
+    hgrad = [
+        [0.25 * signed_sum(disp[c], [signs(a)[k] for a in range(8)]) for c in range(3)]
+        for k in range(3)
+    ]
+    volume = hgrad[0][0] + hgrad[1][1] + hgrad[2][2]
+    square = stiffening * volume * volume
+    lam = 1.0 + square - 2.0 / 3.0
+    press = volume + square * volume / 3.0 - 2.0 / 3.0 * volume
+    quarter = 0.25 * omega
+
+    force = jnp.zeros((LANES, modes), jnp.float32)
+    for c in range(3):
+        stress = [
+            hgrad[k][c] + hgrad[c][k] + press if k == c else hgrad[k][c] + hgrad[c][k]
+            for k in range(3)
+        ]
+        wforce = jnp.concatenate(
+            [quarter * (signed_sum(stress, signs(a)) + disp[c][a]) for a in range(8)], axis=0
+        ).astype(jnp.bfloat16)
+        force = force + lax.dot_general(
+            wforce, v_ref[c], (((0,), (0,)), ((), ())), preferred_element_type=jnp.float32
+        )
+
+    for q in range(modes // LANES):
+        lanes = pl.ds(q * LANES, LANES)
+        grad = [
+            [g_ref[c, pl.ds(k * elements, elements), lanes] for c in range(3)] for k in range(3)
+        ]
+        trace = lam * (grad[0][0] + grad[1][1] + grad[2][2])
+        for c in range(3):
+            terms = [
+                quarter * (grad[k][c] + grad[c][k] + trace if k == c else grad[k][c] + grad[c][k])
+                for k in range(3)
+            ]
+            for a in range(4):
+                half = signed_sum(terms, signs(a))
+                for corner, image in ((a, half), (7 - a, -half)):
+                    at = pl.ds(corner * elements, elements)
+                    w_ref[c, at, lanes] = (
+                        image + quarter * v_ref[c, at, lanes].astype(jnp.float32)
+                    ).astype(jnp.bfloat16)
+
+    for q in range(modes // LANES):
+        lanes = pl.ds(q * LANES, LANES)
+        to_y, to_core = q // 2, q % 2
+        block = jnp.dot(vt_ref[0], w_ref[0, :, lanes], preferred_element_type=jnp.float32)
+        for c in (1, 2):
+            block = block + jnp.dot(
+                vt_ref[c], w_ref[c, :, lanes], preferred_element_type=jnp.float32
+            )
+        tail = force[:8, q * LANES : (q + 1) * LANES]
+        for dest in range(devs):
+            to_x, to_z = dest % 2, dest // 2
+            p, zz = to_z // (planes // 2), to_z % (planes // 2)
+            f, s = (to_y, to_x) if p == 0 else (to_x, to_y)
+            part[p, to_core, f, s, zz, :rows] = block[dest * rows : (dest + 1) * rows]
+            part[p, to_core, f, s, zz, rows:] = tail
+
+    cores = []
+    for p in range(2):
+        copy = pltpu.make_async_remote_copy(
+            src_ref=part.at[p, 1 - core],
+            dst_ref=recv_core.at[p],
+            send_sem=core_send.at[p],
+            recv_sem=core_recv.at[p],
+            device_id=core_peer,
+            device_id_type=MESH,
+        )
+        copy.start()
+        cores.append(copy)
+    order = (((y, y_peer), (x, x_peer)), ((x, x_peer), (y, y_peer)))
+    firsts = []
+    for p in range(2):
+        at, peer = order[p][0]
+        cores[p].wait_recv()
+        mid[p, 1 - at] = part[p, core, 1 - at] + recv_core[p, 1 - at]
+        copy = pltpu.make_async_remote_copy(
+            src_ref=mid.at[p, 1 - at],
+            dst_ref=recv_first.at[p],
+            send_sem=first_send.at[p],
+            recv_sem=first_recv.at[p],
+            device_id=peer,
+            device_id_type=MESH,
+        )
+        copy.start()
+        firsts.append(copy)
+    seconds = []
+    for p in range(2):
+        at = order[p][0][0]
+        there, peer = order[p][1]
+        mid[p, at] = part[p, core, at] + recv_core[p, at]
+        firsts[p].wait_recv()
+        mid[p, at, 1 - there] = mid[p, at, 1 - there] + recv_first[p, 1 - there]
+        copy = pltpu.make_async_remote_copy(
+            src_ref=mid.at[p, at, 1 - there],
+            dst_ref=recv_second.at[p],
+            send_sem=second_send.at[p],
+            recv_sem=second_recv.at[p],
+            device_id=peer,
+            device_id_type=MESH,
+        )
+        copy.start()
+        seconds.append(copy)
+    for p in range(2):
+        at = order[p][0][0]
+        there = order[p][1][0]
+        seconds[p].wait_recv()
+        acc[pl.ds(p * (planes // 2), planes // 2)] = (
+            mid[p, at, there] + recv_first[p, there] + recv_second[p]
+        )
+    lasts = []
+    for step in range(1, planes):
+        dest = lax.rem(z + step, planes)
+        copy = pltpu.make_async_remote_copy(
+            src_ref=acc.at[dest],
+            dst_ref=recv_z.at[step - 1],
+            send_sem=z_send.at[step - 1],
+            recv_sem=z_recv.at[step - 1],
+            device_id=(dest * 2 + x, blk),
+            device_id_type=MESH,
+        )
+        copy.start()
+        lasts.append(copy)
+    count = size_ref[0]
+    for i in range(1, devs):
+        count = count + size_ref[i]
+    scale = lax.rsqrt(jnp.full((8, LANES), 24.0 * count.astype(jnp.float32), jnp.float32))
+    total = acc[z]
+    for step in range(1, planes):
+        lasts[step - 1].wait_recv()
+        total = total + recv_z[step - 1]
+    tangent_ref[...] = total[:rows] * jnp.tile(scale, (rows // 8, 1))
+    residual_ref[...] = (total[rows:] * scale)[:1] - load_ref[...]
+    for copy in cores + firsts + seconds + lasts:
+        copy.wait_send()
+
+
+def fused(devs, basis, send_rows, elem_slot, set_size, elem_weight, element_stiffening, state, load):
+    nodes, _, modes = basis.shape
+    slots = send_rows.shape[2]
+    elements = elem_slot.shape[1]
+    corners = 8 * elements
+    rows = modes // devs
+    half = devs // 4
+    block = (half, rows + 8, LANES)
+    f32, b16 = jnp.float32, jnp.bfloat16
+    dma = pltpu.SemaphoreType.DMA
+    vmem = pl.BlockSpec(memory_space=pltpu.VMEM)
+    smem = pl.BlockSpec(memory_space=pltpu.SMEM)
+    tangent, residual = pl.pallas_call(
+        functools.partial(fused_kernel, devs),
+        out_shape=(
+            jax.ShapeDtypeStruct((rows, LANES), f32),
+            jax.ShapeDtypeStruct((1, LANES), f32),
+        ),
+        in_specs=[vmem, vmem, vmem, smem, vmem, vmem, vmem],
+        out_specs=(vmem, vmem),
+        scratch_shapes=[
+            pltpu.VMEM((3, slots, modes), b16),
+            pltpu.VMEM((3, slots, modes), b16),
+            pltpu.VMEM((3, corners, modes), b16),
+            pltpu.VMEM((3, modes, corners), b16),
+            pltpu.VMEM((3, corners, modes), b16),
+            pltpu.VMEM((3, 3 * elements, modes), f32),
+            pltpu.VMEM((2, 2, 2, 2) + block, f32),
+            pltpu.VMEM((2, 2, 2) + block, f32),
+            pltpu.VMEM((2, 2, 2) + block, f32),
+            pltpu.VMEM((2, 2) + block, f32),
+            pltpu.VMEM((2,) + block, f32),
+            pltpu.VMEM((devs // 2, rows + 8, LANES), f32),
+            pltpu.VMEM((devs // 2 - 1, rows + 8, LANES), f32),
+            dma((devs - 1,)),
+            dma((devs - 1,)),
+            dma((2,)),
+            dma((2,)),
+            dma((2,)),
+            dma((2,)),
+            dma((2,)),
+            dma((2,)),
+            dma((devs // 2 - 1,)),
+            dma((devs // 2 - 1,)),
+        ],
+        compiler_params=pltpu.CompilerParams(
+            collective_id=0, has_side_effects=True, vmem_limit_bytes=40 * 1024 * 1024
+        ),
+        cost_estimate=pl.CostEstimate(
+            flops=6 * modes * modes * corners, bytes_accessed=2 * basis.size, transcendentals=0
+        ),
+        name="galerkin",
+    )(
+        jnp.transpose(basis, (1, 0, 2)),
+        send_rows.reshape(1, slots),
+        elem_slot.reshape(1, corners),
+        set_size,
+        jnp.concatenate([elem_weight, element_stiffening]).reshape(1, 2 * elements),
+        state.reshape(1, modes),
+        load.reshape(1, LANES),
+    )
+    return tangent, residual.reshape(LANES)
+
+
 def solution(mesh):
     in_specs = (
         P("elem", None, None),
@@ -97,4 +434,21 @@
         P("blk"),
     )
     out_specs = (P("elem", "blk"), P("blk"))
-    return jax.shard_map(local, mesh=mesh, in_specs=in_specs, out_specs=out_specs, check_vma=False)
+    devs, blocks = mesh.shape["elem"], mesh.shape["blk"]
+
+    def run(*args):
+        modes, slots, elements = args[0].shape[2], args[1].shape[2], args[2].shape[1] // mesh.size
+        fits = (
+            blocks == 4
+            and modes == blocks * LANES
+            and devs % 4 == 0
+            and modes % (8 * devs) == 0
+            and slots % (16 * devs) == 0
+            and 2 * elements == LANES
+        )
+        part = functools.partial(fused, devs) if fits else local
+        return jax.shard_map(
+            part, mesh=mesh, in_specs=in_specs, out_specs=out_specs, check_vma=False
+        )(*args)
+
+    return run

time: 164 us -> 51.2 us (0.31)
  waiting for transfers between devices: 74.5 us -> 0 us
  Pallas kernels: 0 us -> 43.6 us
  blocking collectives: 27.2 us -> 0 us
  between operations: 15.7 us -> 0.64 us
  matrix products: 11.5 us -> 0 us
  local copies, waits for them, and re-layouts: 17.3 us -> 5.97 us
  other arithmetic: 10.2 us -> 0.75 us
  starting transfers between devices: 7.34 us -> 0 us
    reduce_scatter x2 -> x0, waiting for transfers between devices: 57.5 us -> none  [the longest x1 36.5 us: local(): mine = lax.psum_scatter(halfway, 'elem', scatter_dimension=0, tiled=True)]
    pallas_call x0 -> x1, Pallas kernels: none -> 43.6 us  [fused(): pl.pallas_call(functools.partial(fused_kernel, devs), out_shape=(jax.Shap...]
    psum x1 -> x0, blocking collectives: 21.5 us -> none  [local(): force_cols = lax.psum(force_part, 'elem')]
    all_to_all x1 -> x0, waiting for transfers between devices: 17 us -> none  [local(): lax.all_to_all(outgoing, 'elem', split_axis=0, concat_axis=0, tiled=True)]
    dot_general x7 -> x0, matrix products: 11.5 us -> none  [the longest x1 5.82 us: element_contributions(): jnp.einsum('ak,ekcm->eacm', grads, sym, precision=lax.Precision.HIGHEST)]
    all_to_all x1 -> x0, starting transfers between devices: 7.26 us -> none  [local(): lax.all_to_all(outgoing, 'elem', split_axis=0, concat_axis=0, tiled=True)]
    unnamed x1 -> x0, blocking collectives: 5.73 us -> none
    gather x3 -> x0, local copies, waits for them, and re-layouts: 5.03 us -> none  [the longest x2 3.77 us: local(): chosen_elements = jnp.take(arrived, elem_slot.T.reshape(-1), axis=0)]
  transfers between devices with their start and end apart: 3 -> 0, of which waited for: 3 -> 0; matrix products, arithmetic and copies ran while one was open for 4% -> 0% of each run, Pallas kernels for 0% -> 0%
where the time goes in v1:
time: 51.2 us; the launch traced here: 51 us
  Pallas kernels  43.6 us (85%)
  local copies, waits for them, and re-layouts  5.97 us (12%)
  other arithmetic  0.75 us (1%)
  between operations  0.64 us (1%)
    pallas_call x1, Pallas kernels, fused(): pl.pallas_call(functools.partial(fused_kernel, devs), out_shape=(jax.Shap...  43.6 us
    unnamed x10, local copies, waits for them, and re-layouts  4.52 us

profile of v1, /device:TPU:0, one launch (start us, length us, event | category | flops | bytes accessed | tf_op | source)
XLA Modules:
  0.0 51.0 jit_solution(3925558886057555765)
XLA Ops:
  0.6 0.7 %maximum_bitcast_fusion.aux_ref = f32[1,128]{1,0:T(1,128)S(1)} fusion(f32[64]{0:T(128)} %param.13, f32[64]{0:T(128)} %param.12), kind=kLoop, calls=%fused_computation | loop fusion | flops 128 | bytes 1024 | tf_op jit(solution)/shard_map/reshape | solution.py:418
  1.4 0.8 %reshape.23.slot_ref = s32[1,512]{1,0:T(1,128)S(1)} reshape(s32[8,64]{1,0:T(8,128)} %param.10) | data formatting | bytes 4096 | tf_op jit(solution)/shard_map/reshape | solution.py:416
  2.1 0.7 %reshape.25.state_ref = bf16[1,512]{1,0:T(2,128)(2,1)S(1)} reshape(bf16[512]{0:T(512)(128)(2,1)} %param.14) | data formatting | bytes 2048 | tf_op jit(solution)/shard_map/reshape | solution.py:419
  2.8 0.0 copy-start
  2.8 1.4 %copy-done = bf16[512,3,512]{2,0,1:T(8,128)(2,1)S(1)} copy-done((bf16[512,3,512]{2,0,1:T(8,128)(2,1)S(1)}, bf16[512,3,512]{2,0,1:T(8,128)(2,1)}, u32[]{:S(2)}) %copy-start) | copy-done | bytes 1572888
  4.2 0.0 copy-start.1
  4.2 0.7 %copy-done.1 = s32[1,1,256]{2,1,0:T(1,128)S(1)} copy-done((s32[1,1,256]{2,1,0:T(1,128)S(1)}, s32[1,1,256]{2,1,0:T(1,128)}, u32[]{:S(2)}) %copy-start.1) | copy-done | bytes 1048
  4.9 0.0 copy-start.2
  4.9 0.7 %copy-done.2 = s32[8]{0:T(128)S(1)} copy-done((s32[8]{0:T(128)S(1)}, s32[8]{0:T(128)}, u32[]{:S(2)}) %copy-start.2) | copy-done | bytes 56
  5.6 0.0 copy-start.3
  5.6 0.7 %copy-done.3 = f32[128]{0:T(128)S(1)} copy-done((f32[128]{0:T(128)S(1)}, f32[128]{0:T(128)}, u32[]{:S(2)}) %copy-start.3) | copy-done | bytes 536
  6.2 43.6 %galerkin.1 = (f32[64,128]{1,0:T(8,128)S(1)}, f32[1,128]{1,0:T(1,128)S(1)}) custom-call(bf16[3,512,512]{2,1,0:T(8,128)(2,1)S(1)} %bitcast.6, s32[1,256]{1,0:T(1,128)S(1)} %bitcast.7, s32[1,512]{1,0:T(1,128)S(1)} %reshape.23.slot_ref, s32[8]{0:T(128)S(1)} %copy-done.2, f32[1,128]{1,0:T(1,128)S(1)} %maximum_bitcast_fusion.aux_ref, ...), custom_call_target="tpu_custom_call" | custom-call | flops 805306368 | bytes 1572864 | tf_op jit(solution)/shard_map/galerkin/pallas_call | solution.py:373
  49.8 0.6 %copy.12 = f32[64,128]{1,0:T(8,128)} copy(f32[64,128]{1,0:T(8,128)S(1)} %get-tuple-element.8) | data formatting | bytes 65536
  50.5 0.5 %copy.13 = f32[128]{0:T(128)} copy(f32[128]{0:T(128)S(1)} %bitcast.9) | data formatting | bytes 1024
Async XLA Ops:
  2.8 1.4 %copy-start = (bf16[512,3,512]{2,0,1:T(8,128)(2,1)S(1)}, bf16[512,3,512]{2,0,1:T(8,128)(2,1)}, u32[]{:S(2)}) copy-start(bf16[512,3,512]{2,0,1:T(8,128)(2,1)} %param.8) | copy-start | bytes 4718596
  4.2 0.7 %copy-start.1 = (s32[1,1,256]{2,1,0:T(1,128)S(1)}, s32[1,1,256]{2,1,0:T(1,128)}, u32[]{:S(2)}) copy-start(s32[1,1,256]{2,1,0:T(1,128)} %param.9) | copy-start | bytes 3076
  4.9 0.7 %copy-start.2 = (s32[8]{0:T(128)S(1)}, s32[8]{0:T(128)}, u32[]{:S(2)}) copy-start(s32[8]{0:T(128)} %size_ref.1) | copy-start | bytes 100
  5.6 0.7 %copy-start.3 = (f32[128]{0:T(128)S(1)}, f32[128]{0:T(128)}, u32[]{:S(2)}) copy-start(f32[128]{0:T(128)} %param.15) | copy-start | bytes 1540

commit v2 on v1

--- a/solution.py
+++ b/solution.py
@@ -105,21 +105,32 @@
 
 def fused_kernel(
     devs,
+    basis_hbm,
+    send_hbm,
+    slot_hbm,
+    size_hbm,
+    weight_hbm,
+    stiff_hbm,
+    state_hbm,
+    load_hbm,
+    tangent_ref,
+    residual_ref,
     basis_ref,
     send_ref,
     slot_ref,
     size_ref,
-    aux_ref,
+    weight_ref,
+    stiff_ref,
     state_ref,
     load_ref,
-    tangent_ref,
-    residual_ref,
+    in_sem,
     out_rows,
     arr,
     v_ref,
     vt_ref,
     w_ref,
     g_ref,
+    force_ref,
     part,
     recv_core,
     mid,
@@ -142,7 +153,7 @@
     modes = basis_ref.shape[2]
     slots = arr.shape[1]
     cap = slots // devs
-    elements = aux_ref.shape[1] // 2
+    elements = weight_ref.shape[1]
     corners = 8 * elements
     planes = devs // 2
     rows = modes // devs
@@ -154,6 +165,33 @@
     y_peer = (me, (1 - y) * 2 + core)
     x_peer = (z * 2 + 1 - x, blk)
 
+    def flipped(mask):
+        dest, bit = 0, 1
+        while bit < devs:
+            low = lax.rem(me // bit, 2)
+            dest = dest + bit * (1 - low if mask & bit else low)
+            bit *= 2
+        return dest
+
+    loads = []
+    for i, (src, dst) in enumerate(
+        (
+            (send_hbm, send_ref),
+            (basis_hbm.at[0], basis_ref.at[0]),
+            (basis_hbm.at[1], basis_ref.at[1]),
+            (basis_hbm.at[2], basis_ref.at[2]),
+            (slot_hbm, slot_ref),
+            (size_hbm, size_ref),
+            (weight_hbm, weight_ref),
+            (stiff_hbm, stiff_ref),
+            (state_hbm, state_ref),
+            (load_hbm, load_ref),
+        )
+    ):
+        copy = pltpu.make_async_copy(src, dst, in_sem.at[i])
+        copy.start()
+        loads.append(copy)
+
     barrier = pltpu.get_barrier_semaphore()
     for step in range(1, devs):
         pl.semaphore_signal(
@@ -162,32 +200,38 @@
     for peer in (core_peer, y_peer):
         pl.semaphore_signal(barrier, inc=1, device_id=peer, device_id_type=MESH)
 
+    loads[0].wait()
     asked = jnp.broadcast_to(send_ref[...], (nodes, slots))
     pick_t = jnp.where(lax.broadcasted_iota(jnp.int32, (nodes, slots), 0) == asked, 1.0, 0.0)
     pick = jnp.transpose(pick_t).astype(jnp.bfloat16)
+    mine = pl.ds(pl.multiple_of(me * cap, cap), cap)
+    order = list(range(devs - 1, 0, -1))
+    copies = [[], [], []]
     for c in range(3):
+        loads[1 + c].wait()
         out_rows[c] = jnp.dot(
             pick, basis_ref[c], preferred_element_type=jnp.float32
         ).astype(jnp.bfloat16)
-
-    pl.semaphore_wait(barrier, devs + 1)
-    mine = pl.ds(pl.multiple_of(me * cap, cap), cap)
-    copies = []
-    for step in range(1, devs):
-        dest = lax.rem(me + step, devs)
-        copy = pltpu.make_async_remote_copy(
-            src_ref=out_rows.at[:, pl.ds(pl.multiple_of(dest * cap, cap), cap), :],
-            dst_ref=arr.at[:, mine, :],
-            send_sem=gather_send.at[step - 1],
-            recv_sem=gather_recv.at[step - 1],
-            device_id=(dest, blk),
-            device_id_type=MESH,
-        )
-        copy.start()
-        copies.append(copy)
-    arr[:, mine, :] = out_rows[:, mine, :]
-
-    wanted = jnp.broadcast_to(slot_ref[...], (slots, corners))
+        if c == 0:
+            pl.semaphore_wait(barrier, devs + 1)
+        for mask in order:
+            dest = flipped(mask)
+            copy = pltpu.make_async_remote_copy(
+                src_ref=out_rows.at[c, pl.ds(pl.multiple_of(dest * cap, cap), cap), :],
+                dst_ref=arr.at[c, mine, :],
+                send_sem=gather_send.at[c, mask - 1],
+                recv_sem=gather_recv.at[c, mask - 1],
+                device_id=(dest, blk),
+                device_id_type=MESH,
+            )
+            copy.start()
+            copies[c].append(copy)
+        arr[c, mine, :] = out_rows[c, mine, :]
+
+    for copy in loads[4:]:
+        copy.wait()
+    slot_row = jnp.concatenate([slot_ref[a : a + 1, :] for a in range(8)], axis=1)
+    wanted = jnp.broadcast_to(slot_row, (slots, corners))
     spread_t = jnp.where(lax.broadcasted_iota(jnp.int32, (slots, corners), 0) == wanted, 1.0, 0.0)
     spread = jnp.transpose(spread_t)
     spread_t = spread_t.astype(jnp.bfloat16)
@@ -196,7 +240,8 @@
         [0.25 * signed_sum(by_corner, [signs(a)[k] for a in range(8)]) for k in range(3)], axis=0
     ).astype(jnp.bfloat16)
     spread = spread.astype(jnp.bfloat16)
-    columns = jnp.transpose(jnp.broadcast_to(aux_ref[...], (LANES, 2 * elements)))
+    both = jnp.concatenate([weight_ref[...], stiff_ref[...]], axis=1)
+    columns = jnp.transpose(jnp.broadcast_to(both, (LANES, 2 * elements)))
     live = size_ref[me]
     position = blk * elements + lax.broadcasted_iota(jnp.int32, (elements, LANES), 0)
     omega = jnp.where(position < live, columns[:elements], 0.0)
@@ -204,11 +249,10 @@
     state_rows = jnp.broadcast_to(state_ref[...].astype(jnp.float32), (LANES, modes)).astype(
         jnp.bfloat16
     )
-    for copy in copies:
-        copy.wait()
-
     disp = []
     for c in range(3):
+        for copy in copies[c]:
+            copy.wait_recv()
         rows_c = arr[c]
         v = jnp.dot(spread, rows_c, preferred_element_type=jnp.float32).astype(jnp.bfloat16)
         v_ref[c] = v
@@ -244,6 +288,7 @@
             wforce, v_ref[c], (((0,), (0,)), ((), ())), preferred_element_type=jnp.float32
         )
 
+    force_ref[...] = force[:8]
     for q in range(modes // LANES):
         lanes = pl.ds(q * LANES, LANES)
         grad = [
@@ -263,15 +308,14 @@
                         image + quarter * v_ref[c, at, lanes].astype(jnp.float32)
                     ).astype(jnp.bfloat16)
 
-    for q in range(modes // LANES):
-        lanes = pl.ds(q * LANES, LANES)
-        to_y, to_core = q // 2, q % 2
+    def fill(to_y, to_core):
+        lanes = pl.ds(pl.multiple_of((to_y * 2 + to_core) * LANES, LANES), LANES)
         block = jnp.dot(vt_ref[0], w_ref[0, :, lanes], preferred_element_type=jnp.float32)
         for c in (1, 2):
             block = block + jnp.dot(
                 vt_ref[c], w_ref[c, :, lanes], preferred_element_type=jnp.float32
             )
-        tail = force[:8, q * LANES : (q + 1) * LANES]
+        tail = force_ref[:, lanes]
         for dest in range(devs):
             to_x, to_z = dest % 2, dest // 2
             p, zz = to_z // (planes // 2), to_z % (planes // 2)
@@ -279,6 +323,8 @@
             part[p, to_core, f, s, zz, :rows] = block[dest * rows : (dest + 1) * rows]
             part[p, to_core, f, s, zz, rows:] = tail
 
+    for to_y in range(2):
+        fill(to_y, 1 - core)
     cores = []
     for p in range(2):
         copy = pltpu.make_async_remote_copy(
@@ -291,6 +337,8 @@
         )
         copy.start()
         cores.append(copy)
+    for to_y in range(2):
+        fill(to_y, core)
     order = (((y, y_peer), (x, x_peer)), ((x, x_peer), (y, y_peer)))
     firsts = []
     for p in range(2):
@@ -354,7 +402,7 @@
         total = total + recv_z[step - 1]
     tangent_ref[...] = total[:rows] * jnp.tile(scale, (rows // 8, 1))
     residual_ref[...] = (total[rows:] * scale)[:1] - load_ref[...]
-    for copy in cores + firsts + seconds + lasts:
+    for copy in sum(copies, []) + cores + firsts + seconds + lasts:
         copy.wait_send()
 
 
@@ -369,22 +417,32 @@
     f32, b16 = jnp.float32, jnp.bfloat16
     dma = pltpu.SemaphoreType.DMA
     vmem = pl.BlockSpec(memory_space=pltpu.VMEM)
-    smem = pl.BlockSpec(memory_space=pltpu.SMEM)
+    anywhere = pl.BlockSpec(memory_space=pl.ANY)
     tangent, residual = pl.pallas_call(
         functools.partial(fused_kernel, devs),
         out_shape=(
             jax.ShapeDtypeStruct((rows, LANES), f32),
             jax.ShapeDtypeStruct((1, LANES), f32),
         ),
-        in_specs=[vmem, vmem, vmem, smem, vmem, vmem, vmem],
+        in_specs=[anywhere] * 8,
         out_specs=(vmem, vmem),
         scratch_shapes=[
+            pltpu.VMEM((3, nodes, modes), b16),
+            pltpu.VMEM((1, slots), jnp.int32),
+            pltpu.VMEM((8, elements), jnp.int32),
+            pltpu.SMEM(set_size.shape, jnp.int32),
+            pltpu.VMEM((1, elements), f32),
+            pltpu.VMEM((1, elements), f32),
+            pltpu.VMEM((1, modes), b16),
+            pltpu.VMEM((1, LANES), f32),
+            dma((10,)),
             pltpu.VMEM((3, slots, modes), b16),
             pltpu.VMEM((3, slots, modes), b16),
             pltpu.VMEM((3, corners, modes), b16),
             pltpu.VMEM((3, modes, corners), b16),
             pltpu.VMEM((3, corners, modes), b16),
             pltpu.VMEM((3, 3 * elements, modes), f32),
+            pltpu.VMEM((8, modes), f32),
             pltpu.VMEM((2, 2, 2, 2) + block, f32),
             pltpu.VMEM((2, 2, 2) + block, f32),
             pltpu.VMEM((2, 2, 2) + block, f32),
@@ -392,8 +450,8 @@
             pltpu.VMEM((2,) + block, f32),
             pltpu.VMEM((devs // 2, rows + 8, LANES), f32),
             pltpu.VMEM((devs // 2 - 1, rows + 8, LANES), f32),
-            dma((devs - 1,)),
-            dma((devs - 1,)),
+            dma((3, devs - 1)),
+            dma((3, devs - 1)),
             dma((2,)),
             dma((2,)),
             dma((2,)),
@@ -404,7 +462,7 @@
             dma((devs // 2 - 1,)),
         ],
         compiler_params=pltpu.CompilerParams(
-            collective_id=0, has_side_effects=True, vmem_limit_bytes=40 * 1024 * 1024
+            collective_id=0, has_side_effects=True, vmem_limit_bytes=60 * 1024 * 1024
         ),
         cost_estimate=pl.CostEstimate(
             flops=6 * modes * modes * corners, bytes_accessed=2 * basis.size, transcendentals=0
@@ -413,9 +471,10 @@
     )(
         jnp.transpose(basis, (1, 0, 2)),
         send_rows.reshape(1, slots),
-        elem_slot.reshape(1, corners),
+        elem_slot,
         set_size,
-        jnp.concatenate([elem_weight, element_stiffening]).reshape(1, 2 * elements),
+        elem_weight.reshape(1, elements),
+        element_stiffening.reshape(1, elements),
         state.reshape(1, modes),
         load.reshape(1, LANES),
     )

time: 51.2 us -> 47.8 us (0.934)
  local copies, waits for them, and re-layouts: 5.97 us -> 3.81 us
  other arithmetic: 0.75 us -> 0 us
    unnamed x10 -> x2, local copies, waits for them, and re-layouts: 4.52 us -> 2.55 us
    reshape x1 -> x0, local copies, waits for them, and re-layouts: 0.76 us -> none  [fused(): elem_slot.reshape(1, corners)]
    reshape x1 -> x0, other arithmetic: 0.75 us -> none  [fused(): jnp.concatenate([elem_weight, element_stiffening]).reshape(1, 2 * elements)]
    reshape x1, local copies, waits for them, and re-layouts: 0.68 us -> 1.26 us  [fused(): state.reshape(1, modes)]
where the time goes in v2:
time: 47.8 us; the launch traced here: 47.6 us
  Pallas kernels  43.1 us (90%)
  local copies, waits for them, and re-layouts  3.81 us (8%)
  between operations  0.64 us (1%)
    pallas_call x1, Pallas kernels, fused(): pl.pallas_call(functools.partial(fused_kernel, devs), out_shape=(jax.Shap...  43.1 us
    unnamed x2, local copies, waits for them, and re-layouts  2.55 us
    reshape x1, local copies, waits for them, and re-layouts, fused(): state.reshape(1, modes)  1.26 us

profile of v2, /device:TPU:0, one launch (start us, length us, event | category | flops | bytes accessed | tf_op | source)
XLA Modules:
  0.0 47.6 jit_solution(14875469233416649432)
XLA Ops:
  0.6 1.3 %reshape.25.state_hbm = bf16[1,512]{1,0:T(2,128)(2,1)} reshape(bf16[512]{0:T(512)(128)(2,1)} %param.14) | data formatting | bytes 2048 | tf_op jit(solution)/shard_map/reshape | solution.py:478
  1.9 43.1 %galerkin.1 = (f32[64,128]{1,0:T(8,128)}, f32[1,128]{1,0:T(1,128)}) custom-call(bf16[3,512,512]{2,1,0:T(8,128)(2,1)} %bitcast.6, s32[1,256]{1,0:T(1,128)} %bitcast.7, s32[8,64]{1,0:T(8,128)} %slot_hbm.1, s32[8]{0:T(128)} %size_hbm.1, f32[1,64]{1,0:T(1,128)} %bitcast.8, f32[1,64]{1,0:T(1,128)} %bitcast.9, bf16[1,512]{1,0:T(2,128)(2,1)} %reshape.25.state_hbm, ...), custom_call_target="tpu_custom_call" | custom-call | flops 805306368 | bytes 1572864 | tf_op jit(solution)/shard_map/galerkin/pallas_call | solution.py:421
  45.0 1.4 %copy.12 = f32[64,128]{1,0:T(8,128)} copy(f32[64,128]{1,0:T(8,128)} %get-tuple-element.8) | data formatting | bytes 65536
  46.4 1.2 %copy.13 = f32[128]{0:T(128)} copy(f32[128]{0:T(128)} %bitcast.11) | data formatting | bytes 1024

commit v3 on v2

v3 whole, which is shorter than its diff:
```python
import functools

import jax
import jax.numpy as jnp
from jax import lax
from jax.experimental import pallas as pl
from jax.experimental.pallas import tpu as pltpu
from jax.sharding import PartitionSpec as P

LANES = 128
MESH = pl.DeviceIdType.MESH


def corner_grads():
    corner = jnp.arange(8)[:, None]
    bit = corner // 2 ** jnp.arange(3)[None, :] % 2
    return (bit * 2 - 1).astype(jnp.float32) * 0.25


def element_contributions(basis_matrix, displacement, stiffening_power):
    grads = corner_grads()
    element_count = basis_matrix.shape[0]
    basis_modes = basis_matrix.shape[2]
    corner_nodes = basis_matrix.reshape(element_count, 8, 3, basis_modes)
    grad_basis = jnp.einsum(
        "ak,eacm->ekcm",
        grads.astype(jnp.bfloat16),
        corner_nodes,
        preferred_element_type=jnp.float32,
    )
    moved = displacement.reshape(8, 3, element_count)
    hgrad = jnp.einsum("ak,ace->kce", grads, moved, precision=lax.Precision.HIGHEST)
    volume = hgrad[0, 0] + hgrad[1, 1] + hgrad[2, 2]
    stiff = 1.0 + stiffening_power * volume**2 - 2.0 / 3.0
    press = volume + stiffening_power * volume**3 / 3.0 - 2.0 / 3.0 * volume
    eye = jnp.eye(3, dtype=jnp.float32)
    stress = hgrad + jnp.transpose(hgrad, (1, 0, 2)) + press[None, None, :] * eye[:, :, None]
    force_vector = (
        jnp.einsum("ak,kce->ace", grads, stress, precision=lax.Precision.HIGHEST).reshape(
            24, element_count
        )
        + 0.25 * displacement
    )
    sym = grad_basis + jnp.transpose(grad_basis, (0, 2, 1, 3))
    trace_basis = grad_basis[:, 0, 0] + grad_basis[:, 1, 1] + grad_basis[:, 2, 2]
    mode_image = jnp.einsum("ak,ekcm->eacm", grads, sym, precision=lax.Precision.HIGHEST)
    mode_image = (
        mode_image
        + stiff[:, None, None, None] * grads[None, :, :, None] * trace_basis[:, None, None, :]
        + 0.25 * corner_nodes.astype(jnp.float32)
    )
    return (mode_image.reshape(element_count, 24, basis_modes), force_vector)


def local(basis, send_rows, elem_slot, set_size, elem_weight, element_stiffening, state, load):
    nodes = basis.shape[0]
    basis_modes = basis.shape[2]
    flat = basis.reshape(nodes, 3 * basis_modes)
    outgoing = jnp.take(flat, send_rows[0, 0], axis=0)
    arrived = lax.all_to_all(outgoing, "elem", split_axis=0, concat_axis=0, tiled=True)
    element_count = elem_slot.shape[1]
    chosen_elements = jnp.take(arrived, elem_slot.T.reshape(-1), axis=0)
    basis_matrix = chosen_elements.reshape(element_count, 24, basis_modes)
    set_index = lax.axis_index("elem")
    block_index = lax.axis_index("blk")
    live = lax.dynamic_index_in_dim(set_size, set_index, keepdims=False)
    position = block_index * element_count + jnp.arange(element_count, dtype=jnp.int32)
    weights = jnp.where(position < live, elem_weight, jnp.zeros_like(elem_weight))
    displacement = jnp.einsum("agd,d->ga", basis_matrix, state, preferred_element_type=jnp.float32)
    mode_image, force_vector = element_contributions(basis_matrix, displacement, element_stiffening)
    weighted_image = (weights[:, None, None] * mode_image).astype(jnp.bfloat16)
    weighted_force = (force_vector * weights[None, :]).astype(jnp.bfloat16)
    tangent = lax.dot_general(
        basis_matrix,
        weighted_image,
        (((0, 1), (0, 1)), ((), ())),
        preferred_element_type=jnp.float32,
    )
    force_all = lax.dot_general(
        basis_matrix,
        weighted_force,
        (((0, 1), (1, 0)), ((), ())),
        preferred_element_type=jnp.float32,
    )
    halfway, force_part = (
        lax.psum_scatter(tangent, "blk", scatter_dimension=1, tiled=True),
        lax.psum_scatter(force_all, "blk", scatter_dimension=0, tiled=True),
    )
    mine = lax.psum_scatter(halfway, "elem", scatter_dimension=0, tiled=True)
    force_cols = lax.psum(force_part, "elem")
    scale = lax.rsqrt(24.0 * jnp.sum(set_size).astype(jnp.float32))
    return (mine * scale, force_cols * scale - load)


def signs(corner):
    return [1.0 if corner >> axis & 1 else -1.0 for axis in range(3)]


def signed_sum(terms, sign):
    total = terms[0] if sign[0] > 0 else -terms[0]
    for term, one in zip(terms[1:], sign[1:]):
        total = total + term if one > 0 else total - term
    return total


def fused_kernel(
    devs,
    basis_hbm,
    send_hbm,
    slot_hbm,
    size_hbm,
    weight_hbm,
    stiff_hbm,
    state_hbm,
    load_hbm,
    tangent_ref,
    residual_ref,
    basis_ref,
    send_ref,
    slot_ref,
    size_ref,
    weight_ref,
    stiff_ref,
    state_ref,
    load_ref,
    out_rows,
    arr,
    disp_out,
    disp_in,
    vt_ref,
    w_ref,
    part,
    recv_core,
    mid,
    recv_first,
    recv_second,
    acc,
    recv_z,
    in_sem,
    gather_send,
    gather_recv,
    disp_send,
    disp_recv,
    core_send,
    core_recv,
    first_send,
    first_recv,
    second_send,
    second_recv,
    z_send,
    z_recv,
):
    nodes = basis_ref.shape[1]
    modes = basis_ref.shape[2]
    slots = arr.shape[1]
    cap = slots // devs
    elements = weight_ref.shape[1]
    corners = 8 * elements
    planes = devs // 2
    rows = modes // devs
    chunks = modes // LANES
    f32, b16 = jnp.float32, jnp.bfloat16
    me = lax.axis_index("elem")
    blk = lax.axis_index("blk")
    x, z = lax.rem(me, 2), me // 2
    core, y = lax.rem(blk, 2), blk // 2
    core_peer = (me, y * 2 + 1 - core)
    y_peer = (me, (1 - y) * 2 + core)
    x_peer = (z * 2 + 1 - x, blk)

    def flipped(mask):
        dest, bit = 0, 1
        while bit < devs:
            low = lax.rem(me // bit, 2)
            dest = dest + bit * (1 - low if mask & bit else low)
            bit *= 2
        return dest

    def remote(src, dst, send, recv, peer):
        copy = pltpu.make_async_remote_copy(
            src_ref=src,
            dst_ref=dst,
            send_sem=send,
            recv_sem=recv,
            device_id=peer,
            device_id_type=MESH,
        )
        copy.start()
        return copy

    loads = []
    for i, (src, dst) in enumerate(
        (
            (send_hbm, send_ref),
            (basis_hbm, basis_ref),
            (state_hbm, state_ref),
            (slot_hbm, slot_ref),
            (size_hbm, size_ref),
            (weight_hbm, weight_ref),
            (stiff_hbm, stiff_ref),
            (load_hbm, load_ref),
        )
    ):
        copy = pltpu.make_async_copy(src, dst, in_sem.at[i])
        copy.start()
        loads.append(copy)

    barrier = pltpu.get_barrier_semaphore()
    for step in range(1, devs):
        pl.semaphore_signal(
            barrier, inc=1, device_id=(lax.rem(me + step, devs), blk), device_id_type=MESH
        )
    for peer in (core_peer, y_peer):
        pl.semaphore_signal(barrier, inc=1, device_id=peer, device_id_type=MESH)

    loads[0].wait()
    asked = jnp.broadcast_to(send_ref[...], (nodes, slots))
    pick_t = jnp.where(lax.broadcasted_iota(jnp.int32, (nodes, slots), 0) == asked, 1.0, 0.0)
    pick = jnp.transpose(pick_t).astype(b16)
    mine = pl.ds(pl.multiple_of(me * cap, cap), cap)
    masks = list(range(devs - 1, 0, -1))
    gathers = [[] for _ in range(chunks)]

    def choose(q):
        lanes = pl.ds(q * LANES, LANES)
        for c in range(3):
            out_rows[q, :, c * LANES : (c + 1) * LANES] = jnp.dot(
                pick, basis_ref[c, :, lanes], preferred_element_type=f32
            ).astype(b16)

    def send(q):
        for mask in masks:
            dest = flipped(mask)
            theirs = pl.ds(pl.multiple_of(dest * cap, cap), cap)
            gathers[q].append(
                remote(
                    out_rows.at[q, theirs, :],
                    arr.at[q, mine, :],
                    gather_send.at[q, mask - 1],
                    gather_recv.at[q, mask - 1],
                    (dest, blk),
                )
            )
        arr[q, mine, :] = out_rows[q, mine, :]

    loads[1].wait()
    choose(0)
    pl.semaphore_wait(barrier, devs + 1)
    send(0)
    for q in range(1, chunks):
        choose(q)

    loads[2].wait()
    state = jnp.broadcast_to(state_ref[...].astype(f32).reshape(1, modes), (8, modes))
    component = lax.broadcasted_iota(jnp.int32, (8, modes), 0)
    moved = jnp.zeros((8, slots), f32)
    for c in range(3):
        state_c = jnp.where(component == c, state, 0.0).astype(b16)
        for q in range(chunks):
            moved = moved + lax.dot_general(
                state_c[:, q * LANES : (q + 1) * LANES],
                out_rows[q, :, c * LANES : (c + 1) * LANES],
                (((1,), (1,)), ((), ())),
                preferred_element_type=f32,
            )
    for tile in range(slots // LANES):
        disp_out[tile] = moved[:, tile * LANES : (tile + 1) * LANES]
    disps = []
    for mask in masks:
        dest = flipped(mask)
        disps.append(
            remote(
                disp_out.at[dest * cap // LANES],
                disp_in.at[me],
                disp_send.at[mask - 1],
                disp_recv.at[mask - 1],
                (dest, blk),
            )
        )
    disp_in[me] = disp_out[me * cap // LANES]
    for q in range(1, chunks):
        send(q)

    for copy in loads[3:]:
        copy.wait()
    slot_row = jnp.concatenate([slot_ref[a : a + 1, :] for a in range(8)], axis=1)
    wanted = jnp.broadcast_to(slot_row, (slots, corners))
    spread_t = jnp.where(lax.broadcasted_iota(jnp.int32, (slots, corners), 0) == wanted, 1.0, 0.0)
    spread = jnp.transpose(spread_t)
    spread_t = spread_t.astype(b16)
    by_corner = [spread[a * elements : (a + 1) * elements] for a in range(8)]
    coef = jnp.concatenate(
        [0.25 * signed_sum(by_corner, [signs(a)[k] for a in range(8)]) for k in range(3)], axis=0
    ).astype(b16)
    spread = spread.astype(b16)
    lane_row = slot_row + lax.div(slot_row, cap) * (LANES - cap) + lax.rem(me * cap, LANES)
    wide = (devs * LANES, corners)
    spread_disp = jnp.where(
        lax.broadcasted_iota(jnp.int32, wide, 0) == jnp.broadcast_to(lane_row, wide), 1.0, 0.0
    ).astype(b16)

    for copy in disps:
        copy.wait_recv()
    whole = jnp.concatenate([disp_in[j] for j in range(devs)], axis=1)
    high = whole.astype(b16).astype(f32)
    middle = (whole - high).astype(b16).astype(f32)
    low = whole - high - middle
    pieces = jnp.dot(
        jnp.concatenate([high, middle, low], axis=0).astype(b16),
        spread_disp,
        preferred_element_type=f32,
    )
    picked = pieces[:8] + pieces[8:16] + pieces[16:24]
    disp = [
        [picked[c : c + 1, a * elements : (a + 1) * elements] for a in range(8)] for c in range(3)
    ]
    hgrad = [
        [0.25 * signed_sum(disp[c], [signs(a)[k] for a in range(8)]) for c in range(3)]
        for k in range(3)
    ]
    position = blk * elements + lax.broadcasted_iota(jnp.int32, (1, elements), 1)
    omega = jnp.where(position < size_ref[me], weight_ref[...], 0.0)
    volume = hgrad[0][0] + hgrad[1][1] + hgrad[2][2]
    square = stiff_ref[...] * volume * volume
    lam = 1.0 + square - 2.0 / 3.0
    press = volume + square * volume / 3.0 - 2.0 / 3.0 * volume
    wforce = []
    for c in range(3):
        stress = [
            hgrad[k][c] + hgrad[c][k] + press if k == c else hgrad[k][c] + hgrad[c][k]
            for k in range(3)
        ]
        row = jnp.concatenate(
            [0.25 * omega * (signed_sum(stress, signs(a)) + disp[c][a]) for a in range(8)], axis=1
        )
        wforce.append(jnp.broadcast_to(row, (8, corners)).astype(b16))
    both = jnp.concatenate([0.25 * omega, lam], axis=1)
    columns = jnp.transpose(jnp.broadcast_to(both, (LANES, 2 * elements)))
    quarter, lam = columns[:elements], columns[elements:]

    def place(i, j, block, tail):
        to_y, to_core = j // 2, j % 2
        for to_x in range(2):
            f, s = (to_y, to_x) if i % 2 == 0 else (to_x, to_y)
            part[i, to_core, f, s, :rows] = block[to_x * rows : (to_x + 1) * rows]
            part[i, to_core, f, s, rows:] = tail

    def half_of(ref, i, to_y):
        return ref.at[to_y] if i % 2 == 0 else ref.at[:, to_y]

    tails = []
    cores = [[] for _ in range(planes)]
    for q in range(chunks):
        lanes = pl.ds(q * LANES, LANES)
        for copy in gathers[q]:
            copy.wait_recv()
        arrived = arr[q]
        vt = lax.dot_general(
            arrived, spread_t, (((0,), (0,)), ((), ())), preferred_element_type=f32
        ).astype(b16)
        v = jnp.dot(spread, arrived, preferred_element_type=f32)
        g = jnp.dot(coef, arrived, preferred_element_type=f32)
        grad = [
            [
                g[k * elements : (k + 1) * elements, c * LANES : (c + 1) * LANES]
                for c in range(3)
            ]
            for k in range(3)
        ]
        trace = lam * (grad[0][0] + grad[1][1] + grad[2][2])
        tail = jnp.zeros((8, LANES), f32)
        for c in range(3):
            vt_ref[c, lanes, :] = vt[c * LANES : (c + 1) * LANES]
            v_c = v[:, c * LANES : (c + 1) * LANES]
            terms = [
                grad[k][c] + grad[c][k] + trace if k == c else grad[k][c] + grad[c][k]
                for k in range(3)
            ]
            for a in range(4):
                half = signed_sum(terms, signs(a))
                for corner, image in ((a, half), (7 - a, -half)):
                    at = corner * elements
                    w_ref[c, pl.ds(at, elements), lanes] = (
                        quarter * (image + v_c[at : at + elements])
                    ).astype(b16)
            tail = tail + jnp.dot(wforce[c], v_c.astype(b16), preferred_element_type=f32)
        tails.append(tail)
        down = sum(
            jnp.dot(
                vt_ref[c, : (q + 1) * LANES, :], w_ref[c, :, lanes], preferred_element_type=f32
            )
            for c in range(3)
        )
        for i in range(q + 1):
            place(i, q, down[i * LANES : (i + 1) * LANES], tail)
        if q > 0:
            across = sum(
                jnp.dot(
                    vt_ref[c, lanes, :], w_ref[c, :, : q * LANES], preferred_element_type=f32
                )
                for c in range(3)
            )
            for j in range(q):
                place(q, j, across[:, j * LANES : (j + 1) * LANES], tails[j])
        for i in range(planes):
            for to_y in range(2):
                if max(i, 2 * to_y + 1) == q:
                    cores[i].append(
                        remote(
                            half_of(part.at[i, 1 - core], i, to_y),
                            half_of(recv_core.at[i], i, to_y),
                            core_send.at[i, to_y],
                            core_recv.at[i, to_y],
                            core_peer,
                        )
                    )

    firsts, seconds = [], []
    order = (((y, y_peer), (x, x_peer)), ((x, x_peer), (y, y_peer)))
    for i in range(planes):
        at, peer = order[i % 2][0]
        for copy in cores[i]:
            copy.wait_recv()
        mid[i, 1 - at] = part[i, core, 1 - at] + recv_core[i, 1 - at]
        firsts.append(
            remote(mid.at[i, 1 - at], recv_first.at[i], first_send.at[i], first_recv.at[i], peer)
        )
    for i in range(planes):
        at = order[i % 2][0][0]
        there, peer = order[i % 2][1]
        mid[i, at] = part[i, core, at] + recv_core[i, at]
        firsts[i].wait_recv()
        mid[i, at, 1 - there] = mid[i, at, 1 - there] + recv_first[i, 1 - there]
        seconds.append(
            remote(
                mid.at[i, at, 1 - there],
                recv_second.at[i],
                second_send.at[i],
                second_recv.at[i],
                peer,
            )
        )

    def z_copy(i):
        slot = lax.rem(z - i + planes - 1, planes)
        return pltpu.make_async_remote_copy(
            src_ref=acc.at[i],
            dst_ref=recv_z.at[slot],
            send_sem=z_send.at[i],
            recv_sem=z_recv.at[slot],
            device_id=(i * 2 + x, blk),
            device_id_type=MESH,
        )

    for i in range(planes):
        at = order[i % 2][0][0]
        there = order[i % 2][1][0]
        seconds[i].wait_recv()
        acc[i] = mid[i, at, there] + recv_first[i, there] + recv_second[i]

        @pl.when(z != i)
        def _(i=i):
            z_copy(i).start()

    count = size_ref[0]
    for i in range(1, devs):
        count = count + size_ref[i]
    scale = lax.rsqrt(jnp.full((8, LANES), 24.0 * count.astype(f32), f32))
    total = acc[z]
    for slot in range(planes - 1):
        pltpu.make_async_remote_copy(
            src_ref=acc.at[slot],
            dst_ref=recv_z.at[slot],
            send_sem=z_send.at[slot],
            recv_sem=z_recv.at[slot],
            device_id=x_peer,
            device_id_type=MESH,
        ).wait_recv()
        total = total + recv_z[slot]
    tangent_ref[...] = total[:rows] * jnp.tile(scale, (rows // 8, 1))
    residual_ref[...] = (total[rows:] * scale)[:1] - load_ref[...]
    for copy in sum(gathers, []) + disps + sum(cores, []) + firsts + seconds:
        copy.wait_send()
    for i in range(planes):

        @pl.when(z != i)
        def _(i=i):
            z_copy(i).wait_send()


def fused(devs, basis, send_rows, elem_slot, set_size, elem_weight, element_stiffening, state, load):
    nodes, _, modes = basis.shape
    slots = send_rows.shape[2]
    elements = elem_slot.shape[1]
    corners = 8 * elements
    rows = modes // devs
    planes = devs // 2
    chunks = modes // LANES
    block = (rows + 8, LANES)
    f32, b16 = jnp.float32, jnp.bfloat16
    dma = pltpu.SemaphoreType.DMA
    vmem = pl.BlockSpec(memory_space=pltpu.VMEM)
    anywhere = pl.BlockSpec(memory_space=pl.ANY)
    tangent, residual = pl.pallas_call(
        functools.partial(fused_kernel, devs),
        out_shape=(
            jax.ShapeDtypeStruct((rows, LANES), f32),
            jax.ShapeDtypeStruct((1, LANES), f32),
        ),
        in_specs=[anywhere] * 8,
        out_specs=(vmem, vmem),
        scratch_shapes=[
            pltpu.VMEM((3, nodes, modes), b16),
            pltpu.VMEM((1, slots), jnp.int32),
            pltpu.VMEM((8, elements), jnp.int32),
            pltpu.SMEM(set_size.shape, jnp.int32),
            pltpu.VMEM((1, elements), f32),
            pltpu.VMEM((1, elements), f32),
            pltpu.VMEM((modes,), b16),
            pltpu.VMEM((1, LANES), f32),
            pltpu.VMEM((chunks, slots, 3 * LANES), b16),
            pltpu.VMEM((chunks, slots, 3 * LANES), b16),
            pltpu.VMEM((slots // LANES, 8, LANES), f32),
            pltpu.VMEM((devs, 8, LANES), f32),
            pltpu.VMEM((3, modes, corners), b16),
            pltpu.VMEM((3, corners, modes), b16),
            pltpu.VMEM((planes, 2, 2, 2) + block, f32),
            pltpu.VMEM((planes, 2, 2) + block, f32),
            pltpu.VMEM((planes, 2, 2) + block, f32),
            pltpu.VMEM((planes, 2) + block, f32),
            pltpu.VMEM((planes,) + block, f32),
            pltpu.VMEM((planes,) + block, f32),
            pltpu.VMEM((planes - 1,) + block, f32),
            dma((8,)),
            dma((chunks, devs - 1)),
            dma((chunks, devs - 1)),
            dma((devs - 1,)),
            dma((devs - 1,)),
            dma((planes, 2)),
            dma((planes, 2)),
            dma((planes,)),
            dma((planes,)),
            dma((planes,)),
            dma((planes,)),
            dma((planes,)),
            dma((planes - 1,)),
        ],
        compiler_params=pltpu.CompilerParams(
            collective_id=0, has_side_effects=True, vmem_limit_bytes=60 * 1024 * 1024
        ),
        cost_estimate=pl.CostEstimate(
            flops=6 * modes * modes * corners, bytes_accessed=2 * basis.size, transcendentals=0
        ),
        name="galerkin",
    )(
        jnp.transpose(basis, (1, 0, 2)),
        send_rows.reshape(1, slots),
        elem_slot,
        set_size,
        elem_weight.reshape(1, elements),
        element_stiffening.reshape(1, elements),
        state,
        load.reshape(1, LANES),
    )
    return tangent, residual.reshape(LANES)


def solution(mesh):
    in_specs = (
        P("elem", None, None),
        P("elem", "blk", None),
        P(None, ("elem", "blk")),
        P(),
        P(("elem", "blk")),
        P(("elem", "blk")),
        P(),
        P("blk"),
    )
    out_specs = (P("elem", "blk"), P("blk"))
    devs, blocks = mesh.shape["elem"], mesh.shape["blk"]

    def run(*args):
        modes, slots, elements = args[0].shape[2], args[1].shape[2], args[2].shape[1] // mesh.size
        fits = (
            blocks == 4
            and modes == blocks * LANES
            and devs == 2 * blocks
            and modes % (8 * devs) == 0
            and slots % (16 * devs) == 0
            and 2 * elements == LANES
            and slots % LANES == 0
            and LANES % (slots // devs) == 0
        )
        part = functools.partial(fused, devs) if fits else local
        return jax.shard_map(
            part, mesh=mesh, in_specs=in_specs, out_specs=out_specs, check_vma=False
        )(*args)

    return run
```

time: 47.8 us -> 43.4 us (0.908)
  Pallas kernels: 43.1 us -> 40 us
  local copies, waits for them, and re-layouts: 3.81 us -> 2.55 us
    pallas_call x1, Pallas kernels: 43.1 us -> 40 us  [fused(): pl.pallas_call(functools.partial(fused_kernel, devs), out_shape=(jax.Shap...]
    reshape x1 -> x0, local copies, waits for them, and re-layouts: 1.26 us -> none  [fused(): state.reshape(1, modes)]
where the time goes in v3:
time: 43.4 us; the launch traced here: 43.2 us
  Pallas kernels  40 us (92%)
  local copies, waits for them, and re-layouts  2.55 us (6%)
  between operations  0.64 us (1%)
    pallas_call x1, Pallas kernels, fused(): pl.pallas_call(functools.partial(fused_kernel, devs), out_shape=(jax.Shap...  40 us
    unnamed x2, local copies, waits for them, and re-layouts  2.55 us

profile of v3, /device:TPU:0, one launch (start us, length us, event | category | flops | bytes accessed | tf_op | source)
XLA Modules:
  0.0 43.2 jit_solution(16893853140026742633)
XLA Ops:
  0.6 40.0 %galerkin.1 = (f32[64,128]{1,0:T(8,128)}, f32[1,128]{1,0:T(1,128)}) custom-call(bf16[3,512,512]{2,1,0:T(8,128)(2,1)} %bitcast.6, s32[1,256]{1,0:T(1,128)} %bitcast.7, s32[8,64]{1,0:T(8,128)} %slot_hbm.1, s32[8]{0:T(128)} %size_hbm.1, f32[1,64]{1,0:T(1,128)} %bitcast.8, f32[1,64]{1,0:T(1,128)} %bitcast.9, bf16[512]{0:T(512)(128)(2,1)} %state_hbm.1, ...), custom_call_target="tpu_custom_call" | custom-call | flops 805306368 | bytes 1572864 | tf_op jit(solution)/shard_map/galerkin/pallas_call | solution.py:504
  40.6 1.4 %copy.12 = f32[64,128]{1,0:T(8,128)} copy(f32[64,128]{1,0:T(8,128)} %get-tuple-element.8) | data formatting | bytes 65536
  42.0 1.2 %copy.13 = f32[128]{0:T(128)} copy(f32[128]{0:T(128)} %bitcast.11) | data formatting | bytes 1024

commit v4 on v3

--- a/solution.py
+++ b/solution.py
@@ -188,11 +188,17 @@
         copy.start()
         return copy
 
+    def by_lanes(q):
+        return pl.ds(q * LANES, LANES)
+
     loads = []
     for i, (src, dst) in enumerate(
         (
             (send_hbm, send_ref),
-            (basis_hbm, basis_ref),
+            *(
+                (basis_hbm.at[:, :, by_lanes(q)], basis_ref.at[:, :, by_lanes(q)])
+                for q in range(chunks)
+            ),
             (state_hbm, state_ref),
             (slot_hbm, slot_ref),
             (size_hbm, size_ref),
@@ -222,7 +228,8 @@
     gathers = [[] for _ in range(chunks)]
 
     def choose(q):
-        lanes = pl.ds(q * LANES, LANES)
+        loads[1 + q].wait()
+        lanes = by_lanes(q)
         for c in range(3):
             out_rows[q, :, c * LANES : (c + 1) * LANES] = jnp.dot(
                 pick, basis_ref[c, :, lanes], preferred_element_type=f32
@@ -243,14 +250,13 @@
             )
         arr[q, mine, :] = out_rows[q, mine, :]
 
-    loads[1].wait()
     choose(0)
     pl.semaphore_wait(barrier, devs + 1)
     send(0)
     for q in range(1, chunks):
         choose(q)
 
-    loads[2].wait()
+    loads[1 + chunks].wait()
     state = jnp.broadcast_to(state_ref[...].astype(f32).reshape(1, modes), (8, modes))
     component = lax.broadcasted_iota(jnp.int32, (8, modes), 0)
     moved = jnp.zeros((8, slots), f32)
@@ -281,7 +287,7 @@
     for q in range(1, chunks):
         send(q)
 
-    for copy in loads[3:]:
+    for copy in loads[2 + chunks :]:
         copy.wait()
     slot_row = jnp.concatenate([slot_ref[a : a + 1, :] for a in range(8)], axis=1)
     wanted = jnp.broadcast_to(slot_row, (slots, corners))
@@ -341,17 +347,48 @@
     def place(i, j, block, tail):
         to_y, to_core = j // 2, j % 2
         for to_x in range(2):
-            f, s = (to_y, to_x) if i % 2 == 0 else (to_x, to_y)
+            f, s = (to_y, to_x) if i == planes - 1 else (to_x, to_y)
             part[i, to_core, f, s, :rows] = block[to_x * rows : (to_x + 1) * rows]
             part[i, to_core, f, s, rows:] = tail
 
     def half_of(ref, i, to_y):
-        return ref.at[to_y] if i % 2 == 0 else ref.at[:, to_y]
+        return ref.at[to_y] if i == planes - 1 else ref.at[:, to_y]
+
+    def to_other_core(q, which):
+        for i in which:
+            for to_y in range(2):
+                if max(i, 2 * to_y + 1) == q:
+                    cores[i].append(
+                        remote(
+                            half_of(part.at[i, 1 - core], i, to_y),
+                            half_of(recv_core.at[i], i, to_y),
+                            core_send.at[i, to_y],
+                            core_recv.at[i, to_y],
+                            core_peer,
+                        )
+                    )
+
+    def first(i, to_y):
+        mid[i, 1 - x, to_y] = part[i, core, 1 - x, to_y] + recv_core[i, 1 - x, to_y]
+        firsts[i].append(
+            remote(
+                mid.at[i, 1 - x, to_y],
+                recv_first.at[i, to_y],
+                first_send.at[i, to_y],
+                first_recv.at[i, to_y],
+                x_peer,
+            )
+        )
 
     tails = []
     cores = [[] for _ in range(planes)]
+    firsts = [[] for _ in range(planes)]
     for q in range(chunks):
         lanes = pl.ds(q * LANES, LANES)
+        if q == chunks - 1:
+            for i in range(planes - 1):
+                cores[i][0].wait_recv()
+                first(i, 0)
         for copy in gathers[q]:
             copy.wait_recv()
         arrived = arr[q]
@@ -393,6 +430,7 @@
         )
         for i in range(q + 1):
             place(i, q, down[i * LANES : (i + 1) * LANES], tail)
+        to_other_core(q, range(q))
         if q > 0:
             across = sum(
                 jnp.dot(
@@ -402,34 +440,33 @@
             )
             for j in range(q):
                 place(q, j, across[:, j * LANES : (j + 1) * LANES], tails[j])
-        for i in range(planes):
-            for to_y in range(2):
-                if max(i, 2 * to_y + 1) == q:
-                    cores[i].append(
-                        remote(
-                            half_of(part.at[i, 1 - core], i, to_y),
-                            half_of(recv_core.at[i], i, to_y),
-                            core_send.at[i, to_y],
-                            core_recv.at[i, to_y],
-                            core_peer,
-                        )
-                    )
-
-    firsts, seconds = [], []
-    order = (((y, y_peer), (x, x_peer)), ((x, x_peer), (y, y_peer)))
+            to_other_core(q, (q,))
+
+    for i in range(planes - 1):
+        cores[i][1].wait_recv()
+        first(i, 1)
+    at, peer = y, y_peer
+    last = planes - 1
+    for copy in cores[last]:
+        copy.wait_recv()
+    mid[last, 1 - at] = part[last, core, 1 - at] + recv_core[last, 1 - at]
+    firsts[last].append(
+        remote(
+            mid.at[last, 1 - at],
+            recv_first.at[last],
+            first_send.at[last, 0],
+            first_recv.at[last, 0],
+            peer,
+        )
+    )
+    seconds = []
+    order = [((x, x_peer), (y, y_peer))] * (planes - 1) + [((y, y_peer), (x, x_peer))]
     for i in range(planes):
-        at, peer = order[i % 2][0]
-        for copy in cores[i]:
+        at = order[i][0][0]
+        there, peer = order[i][1]
+        mid[i, at] = part[i, core, at] + recv_core[i, at]
+        for copy in firsts[i]:
             copy.wait_recv()
-        mid[i, 1 - at] = part[i, core, 1 - at] + recv_core[i, 1 - at]
-        firsts.append(
-            remote(mid.at[i, 1 - at], recv_first.at[i], first_send.at[i], first_recv.at[i], peer)
-        )
-    for i in range(planes):
-        at = order[i % 2][0][0]
-        there, peer = order[i % 2][1]
-        mid[i, at] = part[i, core, at] + recv_core[i, at]
-        firsts[i].wait_recv()
         mid[i, at, 1 - there] = mid[i, at, 1 - there] + recv_first[i, 1 - there]
         seconds.append(
             remote(
@@ -453,8 +490,8 @@
         )
 
     for i in range(planes):
-        at = order[i % 2][0][0]
-        there = order[i % 2][1][0]
+        at = order[i][0][0]
+        there = order[i][1][0]
         seconds[i].wait_recv()
         acc[i] = mid[i, at, there] + recv_first[i, there] + recv_second[i]
 
@@ -479,13 +516,24 @@
         total = total + recv_z[slot]
     tangent_ref[...] = total[:rows] * jnp.tile(scale, (rows // 8, 1))
     residual_ref[...] = (total[rows:] * scale)[:1] - load_ref[...]
-    for copy in sum(gathers, []) + disps + sum(cores, []) + firsts + seconds:
+    for copy in sum(gathers, []) + disps + sum(cores, []) + sum(firsts, []) + seconds:
         copy.wait_send()
     for i in range(planes):
 
         @pl.when(z != i)
         def _(i=i):
             z_copy(i).wait_send()
+
+
+def hand_on(tangent_ref, residual_ref, tangent_out, residual_out, sem):
+    copies = [
+        pltpu.make_async_copy(tangent_ref, tangent_out, sem.at[0]),
+        pltpu.make_async_copy(residual_ref, residual_out, sem.at[1]),
+    ]
+    for copy in copies:
+        copy.start()
+    for copy in copies:
+        copy.wait()
 
 
 def fused(devs, basis, send_rows, elem_slot, set_size, elem_weight, element_stiffening, state, load):
@@ -531,15 +579,15 @@
             pltpu.VMEM((planes,) + block, f32),
             pltpu.VMEM((planes,) + block, f32),
             pltpu.VMEM((planes - 1,) + block, f32),
-            dma((8,)),
+            dma((7 + chunks,)),
             dma((chunks, devs - 1)),
             dma((chunks, devs - 1)),
             dma((devs - 1,)),
             dma((devs - 1,)),
             dma((planes, 2)),
             dma((planes, 2)),
-            dma((planes,)),
-            dma((planes,)),
+            dma((planes, 2)),
+            dma((planes, 2)),
             dma((planes,)),
             dma((planes,)),
             dma((planes,)),
@@ -562,6 +610,18 @@
         state,
         load.reshape(1, LANES),
     )
+    tangent, residual = pl.pallas_call(
+        hand_on,
+        out_shape=(
+            jax.ShapeDtypeStruct(tangent.shape, f32),
+            jax.ShapeDtypeStruct(residual.shape, f32),
+        ),
+        in_specs=[anywhere] * 2,
+        out_specs=(anywhere, anywhere),
+        scratch_shapes=[dma((2,))],
+        compiler_params=pltpu.CompilerParams(vmem_limit_bytes=60 * 1024 * 1024),
+        name="hand_on",
+    )(tangent, residual)
     return tangent, residual.reshape(LANES)
 
 

time: 43.4 us -> 44.2 us (1.018)
  Pallas kernels: 40 us -> 43.4 us
  local copies, waits for them, and re-layouts: 2.55 us -> 0 us
    unnamed x2 -> x0, local copies, waits for them, and re-layouts: 2.55 us -> none
    pallas_call x0 -> x1, Pallas kernels: none -> 2.13 us  [fused(): pl.pallas_call(hand_on, out_shape=(jax.ShapeDtypeStruct(tangent.shape, f3...]
    pallas_call x1, Pallas kernels: 40 us -> 41.3 us  [fused(): pl.pallas_call(functools.partial(fused_kernel, devs), out_shape=(jax.Shap...]
where the time goes in v4:
time: 44.2 us; the launch traced here: 44 us
  Pallas kernels  43.4 us (98%)
  between operations  0.64 us (1%)
    pallas_call x1, Pallas kernels, fused(): pl.pallas_call(functools.partial(fused_kernel, devs), out_shape=(jax.Shap...  41.3 us
    pallas_call x1, Pallas kernels, fused(): pl.pallas_call(hand_on, out_shape=(jax.ShapeDtypeStruct(tangent.shape, f3...  2.13 us

profile of v4, /device:TPU:0, one launch (start us, length us, event | category | flops | bytes accessed | tf_op | source)
XLA Modules:
  0.0 44.0 jit_solution(2887146055088367960)
XLA Ops:
  0.6 41.3 %galerkin.1 = (f32[64,128]{1,0:T(8,128)}, f32[1,128]{1,0:T(1,128)}) custom-call(bf16[3,512,512]{2,1,0:T(8,128)(2,1)} %bitcast.6, s32[1,256]{1,0:T(1,128)} %bitcast.7, s32[8,64]{1,0:T(8,128)} %slot_hbm.1, s32[8]{0:T(128)} %size_hbm.1, f32[1,64]{1,0:T(1,128)} %bitcast.8, f32[1,64]{1,0:T(1,128)} %bitcast.9, bf16[512]{0:T(512)(128)(2,1)} %state_hbm.1, ...), custom_call_target="tpu_custom_call" | custom-call | flops 805306368 | bytes 1572864 | tf_op jit(solution)/shard_map/galerkin/pallas_call | solution.py:552
  41.9 2.1 %hand_on.1 = (f32[64,128]{1,0:T(8,128)}, f32[1,128]{1,0:T(1,128)}) custom-call(f32[64,128]{1,0:T(8,128)} %get-tuple-element.6.tangent_ref, f32[1,128]{1,0:T(1,128)} %get-tuple-element.7.residual_ref), custom_call_target="tpu_custom_call" | custom-call | tf_op jit(solution)/shard_map/hand_on/pallas_call | solution.py:613

commit v5 on v4

--- a/solution.py
+++ b/solution.py
@@ -347,12 +347,8 @@
     def place(i, j, block, tail):
         to_y, to_core = j // 2, j % 2
         for to_x in range(2):
-            f, s = (to_y, to_x) if i == planes - 1 else (to_x, to_y)
-            part[i, to_core, f, s, :rows] = block[to_x * rows : (to_x + 1) * rows]
-            part[i, to_core, f, s, rows:] = tail
-
-    def half_of(ref, i, to_y):
-        return ref.at[to_y] if i == planes - 1 else ref.at[:, to_y]
+            part[i, to_core, to_x, to_y, :rows] = block[to_x * rows : (to_x + 1) * rows]
+            part[i, to_core, to_x, to_y, rows:] = tail
 
     def to_other_core(q, which):
         for i in which:
@@ -360,8 +356,8 @@
                 if max(i, 2 * to_y + 1) == q:
                     cores[i].append(
                         remote(
-                            half_of(part.at[i, 1 - core], i, to_y),
-                            half_of(recv_core.at[i], i, to_y),
+                            part.at[i, 1 - core, :, to_y],
+                            recv_core.at[i, :, to_y],
                             core_send.at[i, to_y],
                             core_recv.at[i, to_y],
                             core_peer,
@@ -442,39 +438,24 @@
                 place(q, j, across[:, j * LANES : (j + 1) * LANES], tails[j])
             to_other_core(q, (q,))
 
-    for i in range(planes - 1):
-        cores[i][1].wait_recv()
-        first(i, 1)
-    at, peer = y, y_peer
-    last = planes - 1
-    for copy in cores[last]:
-        copy.wait_recv()
-    mid[last, 1 - at] = part[last, core, 1 - at] + recv_core[last, 1 - at]
-    firsts[last].append(
-        remote(
-            mid.at[last, 1 - at],
-            recv_first.at[last],
-            first_send.at[last, 0],
-            first_recv.at[last, 0],
-            peer,
-        )
-    )
+    for i in range(planes):
+        for to_y in range(len(firsts[i]), 2):
+            cores[i][to_y].wait_recv()
+            first(i, to_y)
     seconds = []
-    order = [((x, x_peer), (y, y_peer))] * (planes - 1) + [((y, y_peer), (x, x_peer))]
-    for i in range(planes):
-        at = order[i][0][0]
-        there, peer = order[i][1]
-        mid[i, at] = part[i, core, at] + recv_core[i, at]
+
+    def second(i):
+        mid[i, x] = part[i, core, x] + recv_core[i, x]
         for copy in firsts[i]:
             copy.wait_recv()
-        mid[i, at, 1 - there] = mid[i, at, 1 - there] + recv_first[i, 1 - there]
+        mid[i, x, 1 - y] = mid[i, x, 1 - y] + recv_first[i, 1 - y]
         seconds.append(
             remote(
-                mid.at[i, at, 1 - there],
+                mid.at[i, x, 1 - y],
                 recv_second.at[i],
                 second_send.at[i],
                 second_recv.at[i],
-                peer,
+                y_peer,
             )
         )
 
@@ -489,15 +470,19 @@
             device_id_type=MESH,
         )
 
-    for i in range(planes):
-        at = order[i][0][0]
-        there = order[i][1][0]
+    def third(i):
         seconds[i].wait_recv()
-        acc[i] = mid[i, at, there] + recv_first[i, there] + recv_second[i]
+        acc[i] = mid[i, x, y] + recv_first[i, y] + recv_second[i]
 
         @pl.when(z != i)
-        def _(i=i):
+        def _():
             z_copy(i).start()
+
+    second(0)
+    for i in range(1, planes):
+        second(i)
+        third(i - 1)
+    third(planes - 1)
 
     count = size_ref[0]
     for i in range(1, devs):

time: 44.2 us -> 44.8 us (1.014)
  Pallas kernels: 43.4 us -> 44 us
    pallas_call x1, Pallas kernels: 41.3 us -> 41.9 us  [fused(): pl.pallas_call(functools.partial(fused_kernel, devs), out_shape=(jax.Shap...]
where the time goes in v5:
time: 44.8 us; the launch traced here: 44.7 us
  Pallas kernels  44 us (98%)
  between operations  0.64 us (1%)
    pallas_call x1, Pallas kernels, fused(): pl.pallas_call(functools.partial(fused_kernel, devs), out_shape=(jax.Shap...  41.9 us
    pallas_call x1, Pallas kernels, fused(): pl.pallas_call(hand_on, out_shape=(jax.ShapeDtypeStruct(tangent.shape, f3...  2.13 us

profile of v5, /device:TPU:0, one launch (start us, length us, event | category | flops | bytes accessed | tf_op | source)
XLA Modules:
  0.0 44.7 jit_solution(14616147872566646757)
XLA Ops:
  0.6 41.9 %galerkin.1 = (f32[64,128]{1,0:T(8,128)}, f32[1,128]{1,0:T(1,128)}) custom-call(bf16[3,512,512]{2,1,0:T(8,128)(2,1)} %bitcast.6, s32[1,256]{1,0:T(1,128)} %bitcast.7, s32[8,64]{1,0:T(8,128)} %slot_hbm.1, s32[8]{0:T(128)} %size_hbm.1, f32[1,64]{1,0:T(1,128)} %bitcast.8, f32[1,64]{1,0:T(1,128)} %bitcast.9, bf16[512]{0:T(512)(128)(2,1)} %state_hbm.1, ...), custom_call_target="tpu_custom_call" | custom-call | flops 805306368 | bytes 1572864 | tf_op jit(solution)/shard_map/galerkin/pallas_call | solution.py:537
  42.5 2.1 %hand_on.1 = (f32[64,128]{1,0:T(8,128)}, f32[1,128]{1,0:T(1,128)}) custom-call(f32[64,128]{1,0:T(8,128)} %get-tuple-element.6.tangent_ref, f32[1,128]{1,0:T(1,128)} %get-tuple-element.7.residual_ref), custom_call_target="tpu_custom_call" | custom-call | tf_op jit(solution)/shard_map/hand_on/pallas_call | solution.py:598

commit v6 on v4

--- a/solution.py
+++ b/solution.py
@@ -347,12 +347,12 @@
     def place(i, j, block, tail):
         to_y, to_core = j // 2, j % 2
         for to_x in range(2):
-            f, s = (to_y, to_x) if i == planes - 1 else (to_x, to_y)
+            f, s = (to_y, to_x) if i % 2 == 0 else (to_x, to_y)
             part[i, to_core, f, s, :rows] = block[to_x * rows : (to_x + 1) * rows]
             part[i, to_core, f, s, rows:] = tail
 
     def half_of(ref, i, to_y):
-        return ref.at[to_y] if i == planes - 1 else ref.at[:, to_y]
+        return ref.at[to_y] if i % 2 == 0 else ref.at[:, to_y]
 
     def to_other_core(q, which):
         for i in which:
@@ -368,27 +368,10 @@
                         )
                     )
 
-    def first(i, to_y):
-        mid[i, 1 - x, to_y] = part[i, core, 1 - x, to_y] + recv_core[i, 1 - x, to_y]
-        firsts[i].append(
-            remote(
-                mid.at[i, 1 - x, to_y],
-                recv_first.at[i, to_y],
-                first_send.at[i, to_y],
-                first_recv.at[i, to_y],
-                x_peer,
-            )
-        )
-
     tails = []
     cores = [[] for _ in range(planes)]
-    firsts = [[] for _ in range(planes)]
     for q in range(chunks):
         lanes = pl.ds(q * LANES, LANES)
-        if q == chunks - 1:
-            for i in range(planes - 1):
-                cores[i][0].wait_recv()
-                first(i, 0)
         for copy in gathers[q]:
             copy.wait_recv()
         arrived = arr[q]
@@ -442,31 +425,21 @@
                 place(q, j, across[:, j * LANES : (j + 1) * LANES], tails[j])
             to_other_core(q, (q,))
 
-    for i in range(planes - 1):
-        cores[i][1].wait_recv()
-        first(i, 1)
-    at, peer = y, y_peer
-    last = planes - 1
-    for copy in cores[last]:
-        copy.wait_recv()
-    mid[last, 1 - at] = part[last, core, 1 - at] + recv_core[last, 1 - at]
-    firsts[last].append(
-        remote(
-            mid.at[last, 1 - at],
-            recv_first.at[last],
-            first_send.at[last, 0],
-            first_recv.at[last, 0],
-            peer,
-        )
-    )
-    seconds = []
-    order = [((x, x_peer), (y, y_peer))] * (planes - 1) + [((y, y_peer), (x, x_peer))]
+    firsts, seconds = [], []
+    order = (((y, y_peer), (x, x_peer)), ((x, x_peer), (y, y_peer)))
     for i in range(planes):
-        at = order[i][0][0]
-        there, peer = order[i][1]
+        at, peer = order[i % 2][0]
+        for copy in cores[i]:
+            copy.wait_recv()
+        mid[i, 1 - at] = part[i, core, 1 - at] + recv_core[i, 1 - at]
+        firsts.append(
+            remote(mid.at[i, 1 - at], recv_first.at[i], first_send.at[i], first_recv.at[i], peer)
+        )
+    for i in range(planes):
+        at = order[i % 2][0][0]
+        there, peer = order[i % 2][1]
         mid[i, at] = part[i, core, at] + recv_core[i, at]
-        for copy in firsts[i]:
-            copy.wait_recv()
+        firsts[i].wait_recv()
         mid[i, at, 1 - there] = mid[i, at, 1 - there] + recv_first[i, 1 - there]
         seconds.append(
             remote(
@@ -490,8 +463,8 @@
         )
 
     for i in range(planes):
-        at = order[i][0][0]
-        there = order[i][1][0]
+        at = order[i % 2][0][0]
+        there = order[i % 2][1][0]
         seconds[i].wait_recv()
         acc[i] = mid[i, at, there] + recv_first[i, there] + recv_second[i]
 
@@ -516,7 +489,7 @@
         total = total + recv_z[slot]
     tangent_ref[...] = total[:rows] * jnp.tile(scale, (rows // 8, 1))
     residual_ref[...] = (total[rows:] * scale)[:1] - load_ref[...]
-    for copy in sum(gathers, []) + disps + sum(cores, []) + sum(firsts, []) + seconds:
+    for copy in sum(gathers, []) + disps + sum(cores, []) + firsts + seconds:
         copy.wait_send()
     for i in range(planes):
 
@@ -586,8 +559,8 @@
             dma((devs - 1,)),
             dma((planes, 2)),
             dma((planes, 2)),
-            dma((planes, 2)),
-            dma((planes, 2)),
+            dma((planes,)),
+            dma((planes,)),
             dma((planes,)),
             dma((planes,)),
             dma((planes,)),

time: 44.2 us -> 43.8 us (level)
  no operation moved by 1% of the time
where the time goes in v6:
time: 43.8 us; the launch traced here: 43.6 us
  Pallas kernels  43 us (98%)
  between operations  0.64 us (1%)
    pallas_call x1, Pallas kernels, fused(): pl.pallas_call(functools.partial(fused_kernel, devs), out_shape=(jax.Shap...  40.8 us
    pallas_call x1, Pallas kernels, fused(): pl.pallas_call(hand_on, out_shape=(jax.ShapeDtypeStruct(tangent.shape, f3...  2.13 us

profile of v6, /device:TPU:0, one launch (start us, length us, event | category | flops | bytes accessed | tf_op | source)
XLA Modules:
  0.0 43.6 jit_solution(14363347150782425569)
XLA Ops:
  0.6 40.8 %galerkin.1 = (f32[64,128]{1,0:T(8,128)}, f32[1,128]{1,0:T(1,128)}) custom-call(bf16[3,512,512]{2,1,0:T(8,128)(2,1)} %bitcast.6, s32[1,256]{1,0:T(1,128)} %bitcast.7, s32[8,64]{1,0:T(8,128)} %slot_hbm.1, s32[8]{0:T(128)} %size_hbm.1, f32[1,64]{1,0:T(1,128)} %bitcast.8, f32[1,64]{1,0:T(1,128)} %bitcast.9, bf16[512]{0:T(512)(128)(2,1)} %state_hbm.1, ...), custom_call_target="tpu_custom_call" | custom-call | flops 805306368 | bytes 1572864 | tf_op jit(solution)/shard_map/galerkin/pallas_call | solution.py:525
  41.5 2.1 %hand_on.1 = (f32[64,128]{1,0:T(8,128)}, f32[1,128]{1,0:T(1,128)}) custom-call(f32[64,128]{1,0:T(8,128)} %get-tuple-element.6.tangent_ref, f32[1,128]{1,0:T(1,128)} %get-tuple-element.7.residual_ref), custom_call_target="tpu_custom_call" | custom-call | tf_op jit(solution)/shard_map/hand_on/pallas_call | solution.py:586

commit v7 on v3

--- a/solution.py
+++ b/solution.py
@@ -486,6 +486,17 @@
         @pl.when(z != i)
         def _(i=i):
             z_copy(i).wait_send()
+
+
+def hand_on(tangent_ref, residual_ref, tangent_out, residual_out, sem):
+    copies = [
+        pltpu.make_async_copy(tangent_ref, tangent_out, sem.at[0]),
+        pltpu.make_async_copy(residual_ref, residual_out, sem.at[1]),
+    ]
+    for copy in copies:
+        copy.start()
+    for copy in copies:
+        copy.wait()
 
 
 def fused(devs, basis, send_rows, elem_slot, set_size, elem_weight, element_stiffening, state, load):
@@ -562,6 +573,18 @@
         state,
         load.reshape(1, LANES),
     )
+    tangent, residual = pl.pallas_call(
+        hand_on,
+        out_shape=(
+            jax.ShapeDtypeStruct(tangent.shape, f32),
+            jax.ShapeDtypeStruct(residual.shape, f32),
+        ),
+        in_specs=[anywhere] * 2,
+        out_specs=(anywhere, anywhere),
+        scratch_shapes=[dma((2,))],
+        compiler_params=pltpu.CompilerParams(vmem_limit_bytes=60 * 1024 * 1024),
+        name="hand_on",
+    )(tangent, residual)
     return tangent, residual.reshape(LANES)
 
 

time: 43.4 us -> 42.9 us (0.988)
  local copies, waits for them, and re-layouts: 2.55 us -> 0 us
  Pallas kernels: 40 us -> 42.1 us
    unnamed x2 -> x0, local copies, waits for them, and re-layouts: 2.55 us -> none
    pallas_call x0 -> x1, Pallas kernels: none -> 2.13 us  [fused(): pl.pallas_call(hand_on, out_shape=(jax.ShapeDtypeStruct(tangent.shape, f3...]
where the time goes in v7:
time: 42.9 us; the launch traced here: 42.7 us
  Pallas kernels  42.1 us (98%)
  between operations  0.64 us (1%)
    pallas_call x1, Pallas kernels, fused(): pl.pallas_call(functools.partial(fused_kernel, devs), out_shape=(jax.Shap...  40 us
    pallas_call x1, Pallas kernels, fused(): pl.pallas_call(hand_on, out_shape=(jax.ShapeDtypeStruct(tangent.shape, f3...  2.13 us

profile of v7, /device:TPU:0, one launch (start us, length us, event | category | flops | bytes accessed | tf_op | source)
XLA Modules:
  0.0 42.7 jit_solution(2242382246811651545)
XLA Ops:
  0.6 40.0 %galerkin.1 = (f32[64,128]{1,0:T(8,128)}, f32[1,128]{1,0:T(1,128)}) custom-call(bf16[3,512,512]{2,1,0:T(8,128)(2,1)} %bitcast.6, s32[1,256]{1,0:T(1,128)} %bitcast.7, s32[8,64]{1,0:T(8,128)} %slot_hbm.1, s32[8]{0:T(128)} %size_hbm.1, f32[1,64]{1,0:T(1,128)} %bitcast.8, f32[1,64]{1,0:T(1,128)} %bitcast.9, bf16[512]{0:T(512)(128)(2,1)} %state_hbm.1, ...), custom_call_target="tpu_custom_call" | custom-call | flops 805306368 | bytes 1572864 | tf_op jit(solution)/shard_map/galerkin/pallas_call | solution.py:515
  40.6 2.1 %hand_on.1 = (f32[64,128]{1,0:T(8,128)}, f32[1,128]{1,0:T(1,128)}) custom-call(f32[64,128]{1,0:T(8,128)} %get-tuple-element.6.tangent_ref, f32[1,128]{1,0:T(1,128)} %get-tuple-element.7.residual_ref), custom_call_target="tpu_custom_call" | custom-call | tf_op jit(solution)/shard_map/hand_on/pallas_call | solution.py:576
